TPU v7x, 32 devices: a whole 2x2x4 slice. The times are simulated.
32 devices in a mesh: seq: 8 (over z, x), batch: 4 (over y, core).
Axes of the slice: x: 2, y: 2, z: 4, core: 2. Of those that a mesh axis runs over, the one named last changes fastest.
Arguments:
- hidden: bfloat16 [4, 2048, 2048], P('batch', 'seq'), may hold values from -6 to 6
- in_weight: bfloat16 [1024, 4352], P('batch'), may hold values from -0.1875 to 0.1875
- dt_weight: bfloat16 [1024, 32], replicated, may hold values from -0.1875 to 0.1875
- conv_weight: float32 [4, 2304], replicated, may hold values from -3 to 3
- conv_bias: float32 [2304], replicated, may hold values from -3 to 3
- dt_bias: float32 [32], replicated, may hold values from -1 to 1
- a_log: float32 [32], replicated
- d_skip: float32 [32], replicated, may hold values from 0.5 to 1.5
- norm_gain: float32 [2048], replicated, may hold values from 0.1 to 1.9
- out_weight: bfloat16 [2048, 1024], P('batch'), may hold values from -0.125 to 0.125
Outputs:
- mixed: bfloat16 [4, 2048, 2048], P('batch', 'seq')
All inputs are finite; a program needn't handle non-finite values.
Results may differ from a plain program's by a relative error of at most 0.0062.
Values may be sent and summed in bfloat16 or wider, within the bound.
A program may use at most 320 MiB of HBM per device.

v0:
```python
import jax
import jax.numpy as jnp
from jax import lax
from jax.sharding import PartitionSpec as P

INNER = 2048
HEADS = 32
STATE = 128
SPAN = 128
HEADDIM = 64


def padded_2(cells, sides, width):
    for axis, dim in sides:
        count = lax.axis_size(axis)
        ends = count - 1
        head = lax.slice_in_dim(cells, 0, width, axis=dim)
        tail = lax.slice_in_dim(cells, cells.shape[dim] - width, cells.shape[dim], axis=dim)
        cells = jnp.concatenate(
            [
                lax.ppermute(tail, axis, [(i, (i + 1) % count) for i in range(ends)]),
                cells,
                lax.ppermute(head, axis, [((i + 1) % count, i) for i in range(ends)]),
            ],
            axis=dim,
        )
    return cells


def entering(part, axis, combine, identity, reverse):
    count = lax.axis_size(axis)
    place = lax.axis_index(axis)
    ahead = count - 1 - place if reverse else place
    gathered = jax.tree.map(lambda a: lax.all_gather(a, axis), part)
    state = jax.tree.map(lambda a, e: jnp.zeros_like(a) + jnp.asarray(e, a.dtype), part, identity)

    def one(lap, state):
        source = count - 1 - lap if reverse else lap
        return combine(
            state, jax.tree.map(lambda a: lax.dynamic_index_in_dim(a, source, 0, False), gathered)
        )

    return lax.fori_loop(0, ahead, one, state)


def contract_rows(activations, weight):
    return jnp.einsum(
        "gtd,dk->gtk",
        activations,
        lax.all_gather(weight, "batch", axis=0, tiled=True),
        preferred_element_type=jnp.float32,
    )


def conv_act(padded, conv_weight, conv_bias, length, reverse):
    running = conv_bias
    for tap_index in range(4):
        offset = 6 - tap_index if reverse else tap_index
        running = running + conv_weight[tap_index] * padded[:, offset : offset + length]
    return jax.nn.silu(running).astype(jnp.bfloat16)


def passing(start_state, growth, states):

    def advance(state_now, inputs):
        growth_step, fresh_state = inputs
        return (growth_step[..., None, None] * state_now + fresh_state, state_now)

    last_state, entries = lax.scan(
        advance, start_state, (jnp.moveaxis(growth, 1, 0), jnp.moveaxis(states, 1, 0))
    )
    return (last_state, jnp.moveaxis(entries, 0, 1))


def span_parts(act, step_dt, decay_rate):
    groups, length = (act.shape[0], act.shape[1])
    span_count = length // SPAN
    values = act[:, :, :INNER].reshape(groups, span_count, SPAN, HEADS, HEADDIM)
    write_vec = act[:, :, INNER : INNER + STATE].reshape(groups, span_count, SPAN, STATE)
    read_vec = act[:, :, INNER + STATE :].reshape(groups, span_count, SPAN, STATE)
    step_rates = step_dt.reshape(groups, HEADS, span_count, SPAN).transpose(0, 2, 1, 3)
    cumulate = jnp.cumsum(step_rates * decay_rate[None, None, :, None], axis=3)
    scores = jnp.einsum("gkqn,gksn->gkqs", read_vec, write_vec, preferred_element_type=jnp.float32)
    causal = lax.broadcasted_iota(jnp.int32, (SPAN, SPAN), 0) >= lax.broadcasted_iota(
        jnp.int32, (SPAN, SPAN), 1
    )
    decay_mask = jnp.exp(
        jnp.where(causal, cumulate[..., :, None] - cumulate[..., None, :], -jnp.inf)
    )
    mixing = (scores[:, :, None] * decay_mask * step_rates[:, :, :, None, :]).astype(jnp.bfloat16)
    within = jnp.einsum("gkhqs,gkshp->gkqhp", mixing, values, preferred_element_type=jnp.float32)
    scaled = jnp.exp(cumulate[..., -1:] - cumulate) * step_rates
    weighted = (write_vec[:, :, None] * scaled[..., None]).astype(jnp.bfloat16)
    states = jnp.einsum("gkshp,gkhsn->gkhpn", values, weighted, preferred_element_type=jnp.float32)
    growth = jnp.exp(cumulate[..., -1])
    return (values, read_vec, cumulate, within, states, growth)


def finish(parts, incoming, d_skip):
    values, read_vec, cumulate, within, states, growth = parts
    groups, span_count = (values.shape[0], values.shape[1])
    _, entries = passing(incoming, growth, states)
    current = entries.astype(jnp.bfloat16)
    from_state = jnp.einsum(
        "gkqn,gkhpn->gkqhp", read_vec, current, preferred_element_type=jnp.float32
    )
    from_state = from_state * jnp.exp(cumulate).transpose(0, 1, 3, 2)[..., None]
    result = within + from_state + d_skip[:, None] * values.astype(jnp.float32)
    return result.reshape(groups, span_count * SPAN, INNER)


def link_pairs(earlier, later_pair):
    return (earlier[0] * later_pair[0], later_pair[0][..., None, None] * earlier[1] + later_pair[1])


def gate_norm(result, gate_part, norm_gain):
    gated = result * jax.nn.silu(gate_part.astype(jnp.float32))
    return gated * lax.rsqrt(jnp.mean(gated * gated, axis=-1, keepdims=True) + 1e-05) * norm_gain


def on_device(
    hidden,
    in_weight,
    dt_weight,
    conv_weight,
    conv_bias,
    dt_bias,
    a_log,
    d_skip,
    norm_gain,
    out_weight,
):
    model_width = hidden.shape[2] // 2
    local_count = hidden.shape[0]
    forward_half = hidden[:, :, :model_width]
    second = jnp.flip(hidden[:, :, model_width:], 2)
    streams = jnp.concatenate([forward_half, second], 0)
    groups, length = (streams.shape[0], streams.shape[1])
    projected = contract_rows(streams, in_weight).astype(jnp.bfloat16)
    gate_part = projected[:, :, :INNER]
    conv_in = projected[:, :, INNER:]
    step_dt = jax.nn.softplus(
        jnp.einsum("gtd,dh->ght", streams, dt_weight, preferred_element_type=jnp.float32)
        + dt_bias[None, :, None]
    )
    padded = padded_2(conv_in, (("seq", 1),), 3)
    ahead_act = conv_act(padded, conv_weight, conv_bias, length, False)
    behind_act = conv_act(padded, conv_weight, conv_bias, length, True)
    decay_rate = -jnp.exp(a_log)
    ahead_parts = span_parts(ahead_act, step_dt, decay_rate)
    behind_parts = span_parts(jnp.flip(behind_act, 1), jnp.flip(step_dt, 2), decay_rate)
    zero_state = jnp.zeros((groups, HEADS, HEADDIM, STATE), jnp.float32)
    unit_decay = jnp.ones((groups, HEADS), jnp.float32)
    ahead_total, _ = passing(zero_state, ahead_parts[5], ahead_parts[4])
    behind_total, _ = passing(zero_state, behind_parts[5], behind_parts[4])
    ahead_pair = (jnp.prod(ahead_parts[5], 1), ahead_total)
    behind_pair = (jnp.prod(behind_parts[5], 1), behind_total)
    ahead_in = entering(ahead_pair, "seq", link_pairs, (unit_decay, zero_state), False)
    behind_in = entering(behind_pair, "seq", link_pairs, (unit_decay, zero_state), True)
    forward_y = finish(ahead_parts, ahead_in[1], d_skip)
    backward_y = jnp.flip(finish(behind_parts, behind_in[1], d_skip), 1)
    combined = (
        gate_norm(forward_y, gate_part, norm_gain) + gate_norm(backward_y, gate_part, norm_gain)
    ).astype(jnp.bfloat16)
    stream_out = contract_rows(combined, out_weight).astype(jnp.bfloat16)
    top_half = stream_out[:local_count]
    low_half = jnp.flip(stream_out[local_count:], 2)
    return jnp.concatenate([top_half, low_half], 2)


def solution(mesh):
    placed = (
        P("batch", "seq", None),
        P("batch", None),
        P(),
        P(),
        P(),
        P(),
        P(),
        P(),
        P(),
        P("batch", None),
    )
    return jax.shard_map(
        on_device, mesh=mesh, in_specs=placed, out_specs=P("batch", "seq", None), check_vma=False
    )
```

profile of v0, /device:TPU:31, one launch (start us, length us, event | category | flops | bytes accessed | tf_op | source)
XLA Modules:
  0.0 678.4 jit_solution(9008485972608331104)
XLA Ops:
  12.5 58.1 %all-gather.11.cloned.1.call-done = bf16[1024,4352]{1,0:T(8,128)(2,1)} async-done(((bf16[256,4352]{1,0:T(8,128)(2,1)}), bf16[1024,4352]{1,0:T(8,128)(2,1)}) %all-gather.11.cloned.1.call-update) | async-done | bytes 8912912 | tf_op jit(solution)/shard_map/all_gather | solution.py:50
  70.6 8.5 %fusion.2 = bf16[2,256,4352]{2,1,0:T(8,128)(2,1)S(1)} fusion(bf16[1024,4352]{1,0:T(8,128)(2,1)} %all-gather.11.cloned.1.call-done, bf16[1,256,1024]{2,1,0:T(8,128)(2,1)S(1)} %rev.17, bf16[1,256,1024]{2,1,0:T(8,128)(2,1)S(1)} %get-tuple-element.393), kind=kOutput, calls=%fused_computation.22 | convolution fusion | flops 4566155264 | bytes 14417920 | tf_op jit(solution)/shard_map/gtd,dk->gtk/dot_general | solution.py:47
  86.3 6.8 %multiply_convert_fusion.4 = (bf16[2,256,2304]{2,1,0:T(8,128)(2,1)S(1)}, bf16[2,256,2304]{2,1,0:T(8,128)(2,1)S(1)}) fusion(bf16[2,256,2304]{2,1,0:T(8,128)(2,1)S(1)} %slice-done, bf16[2,3,2304]{2,1,0:T(4,128)(2,1)S(1)} %collective-permute-done.1, f32[2304]{0:T(1024)S(1)} %get-tuple-element.325, f32[2304]{0:T(1024)S(1)} %get-tuple-element.326, ...), kind=kLoop, calls=%fused_computation.25 | loop fusion | flops 58982400 | bytes 7179264 | tf_op jit(solution)/shard_map/convert_element_type | solution.py:60
  95.5 30.6 %slice.122 = bf16[2,256,2048]{2,1,0:T(8,128)(2,1)} reverse(bf16[2,256,2048]{2,1,0:T(8,128)(2,1)} %slice.146), dimensions={1} | reverse | bytes 4194304 | tf_op jit(solution)/shard_map/slice | solution.py:78
  126.1 7.1 %reshape.121 = bf16[2,2,128,32,64]{4,3,2,1,0:T(8,128)(2,1)} reshape(bf16[2,256,2048]{2,1,0:T(8,128)(2,1)} %slice.122) | data formatting | bytes 4194304 | tf_op jit(solution)/shard_map/reshape | solution.py:78
  133.2 6.5 copy.69
  156.8 7.1 %reshape.120 = bf16[2,2,128,32,64]{4,3,2,1,0:T(8,128)(2,1)} reshape(bf16[2,256,2048]{2,1,0:T(8,128)(2,1)} %slice.136) | data formatting | bytes 4194304 | tf_op jit(solution)/shard_map/reshape | solution.py:78
  163.9 6.8 %copy.57 = bf16[2,2,128,32,64]{2,4,3,1,0:T(8,128)(2,1)} copy(bf16[2,2,128,32,64]{4,3,2,1,0:T(8,128)(2,1)} %reshape.120) | data formatting | bytes 4194304 | tf_op jit(solution)/shard_map/reshape | solution.py:78
  183.6 14.0 %all-gather.5 = f32[8,2,32]{2,1,0:T(2,128)S(1)} all-gather(f32[1,2,32]{2,1,0:T(2,128)S(1)} %bitcast.185), channel_id=4, replica_groups=mesh['seq'=8,'batch'=4] {'seq'}, dimensions={0}, use_global_device_ids=true | all-gather | bytes 2304 | tf_op jit(solution)/shard_map/all_gather | solution.py:34
  197.6 14.1 %all-gather.4 = f32[8,2,32]{2,1,0:T(2,128)S(1)} all-gather(f32[1,2,32]{2,1,0:T(2,128)S(1)} %bitcast.186), channel_id=2, replica_groups=mesh['seq'=8,'batch'=4] {'seq'}, dimensions={0}, use_global_device_ids=true | all-gather | bytes 2304 | tf_op jit(solution)/shard_map/all_gather | solution.py:34
  212.3 6.3 fusion.6
  218.6 161.1 %all-gather.17.cloned.1.call-done = f32[16,32,64,128]{3,2,1,0:T(8,128)} async-done(((f32[2,32,64,128]{3,2,1,0:T(8,128)}), f32[16,32,64,128]{3,2,1,0:T(8,128)}) %all-gather.17.cloned.1.call-update) | async-done | bytes 16777232 | tf_op jit(solution)/shard_map/all_gather | solution.py:34
  381.8 6.0 while.75
  387.8 6.9 %fusion.14 = f32[2,2,128,32,64]{2,4,3,1,0:T(8,128)} fusion(f32[2,2,32,64,128]{4,3,2,1,0:T(8,128)} %fusion.6, bf16[2,2,128,32,64]{2,4,3,1,0:T(8,128)(2,1)} %copy.69, bf16[2,2,128,128,1]{3,2,4,1,0:T(8,128)(2,1)S(1)} %bitcast.178, f32[2,2,128,32]{2,3,1,0:T(8,128)S(1)} %get-tuple-element.395, f32[32]{0:T(128)S(1)} %copy-done.11, ...), kind=kOutput, calls=%fused_computation.38 | convolution fusion | flops 273678336 | bytes 12779648 | tf_op jit(solution)/shard_map/gkqn,gkhpn->gkqhp/dot_general | solution.py:104
  394.7 9.3 %copy.82 = f32[2,2,128,32,64]{4,3,2,1,0:T(8,128)} copy(f32[2,2,128,32,64]{2,4,3,1,0:T(8,128)} %fusion.14) | data formatting | bytes 8388608 | tf_op jit(solution)/shard_map/reshape | solution.py:109
  404.0 7.8 %reshape.119 = f32[2,256,2048]{2,1,0:T(8,128)} reshape(f32[2,2,128,32,64]{4,3,2,1,0:T(8,128)} %copy.82) | data formatting | bytes 8388608 | tf_op jit(solution)/shard_map/reshape | solution.py:109
  411.9 32.6 %rev.19 = f32[2,256,2048]{2,1,0:T(8,128)} reverse(f32[2,256,2048]{2,1,0:T(8,128)} %reshape.119), dimensions={1} | reverse | bytes 8388608 | tf_op jit(solution)/shard_map/jit(_flip)/rev | solution.py:161
  444.5 163.1 %all-gather.15.cloned.1.call-done = f32[16,32,64,128]{3,2,1,0:T(8,128)} async-done(((f32[2,32,64,128]{3,2,1,0:T(8,128)}), f32[16,32,64,128]{3,2,1,0:T(8,128)}) %all-gather.15.cloned.1.call-update) | async-done | bytes 16777232 | tf_op jit(solution)/shard_map/all_gather | solution.py:34
  607.8 14.9 %while.72 = (s32[]{:T(128)}, f32[2,32,64,128]{3,2,1,0:T(8,128)S(1)}, s32[]{:T(128)}, f32[8,2,32]{2,1,0:T(2,128)S(1)}, f32[8,2,32,64,128]{4,3,2,1,0:T(8,128)}, /*index=5*/s32[]{:T(128)}, s32[]{:T(128)}, s32[]{:T(128)}) while((s32[]{:T(128)}, f32[2,32,64,128]{3,2,1,0:T(8,128)S(1)}, s32[]{:T(128)}, f32[8,2,32]{2,1,0:T(2,128)S(1)}, ...), condition=%wide.region_5.6_spmd, body=%wide.region_4.5_spmd.sunk | while | flops 1048581 | bytes 6292351 | solution.py:43
  624.6 6.0 while.73
  638.1 9.1 %copy.81 = f32[2,2,128,32,64]{4,3,2,1,0:T(8,128)} copy(f32[2,2,128,32,64]{2,4,3,1,0:T(8,128)} %fusion.15) | data formatting | bytes 8388608 | tf_op jit(solution)/shard_map/reshape | solution.py:109
  647.3 7.9 %reshape.118 = f32[2,256,2048]{2,1,0:T(8,128)} reshape(f32[2,2,128,32,64]{4,3,2,1,0:T(8,128)} %copy.81) | data formatting | bytes 8388608 | tf_op jit(solution)/shard_map/reshape | solution.py:109
  655.1 5.1 multiply_reduce_fusion.1
  660.3 8.7 %fusion.46 = bf16[2,256,1024]{2,1,0:T(8,128)(2,1)S(1)} fusion(bf16[2048,1024]{1,0:T(8,128)(2,1)} %all-gather.13.cloned.1.call-done, f32[2,256]{1,0:T(2,128)S(1)} %add_rsqrt_fusion, f32[2048]{0:T(1024)S(1)} %copy-done.12, f32[2,256]{1,0:T(2,128)S(1)} %add_rsqrt_fusion.1, f32[2,256,2048]{2,1,0:T(8,128)} %reshape.118, bf16[2,256,4352]{2,1,0:T(8,128)(2,1)} %copy-done.7, ...), kind=kOutput, calls=%fused_computation.82 | convolution fusion | flops 2160590848 | bytes 15740928 | tf_op jit(solution)/shard_map/gtd,dk->gtk/dot_general | solution.py:47
  (133 shorter events, 94.3 us)
Async XLA Ops:
  6.5 3.7 copy-start
  6.5 3.8 copy-start.13
  6.5 4.4 copy-start.14
  6.5 64.1 %all-gather.11.cloned.1.call-start = ((), (), s32[]{:S(2)}) async-start(), calls=%async_computation | async-start | bytes 11141120 | tf_op jit(solution)/shard_map/all_gather | solution.py:50
  7.3 372.4 %all-gather.17.cloned.1.call-start = ((), (), s32[]{:S(2)}) async-start(), calls=%async_computation.3 | async-start | bytes 18874368 | tf_op jit(solution)/shard_map/all_gather | solution.py:34
  12.5 72.0 %copy-start.9 = (f32[4,2304]{1,0:T(4,128)S(1)}, f32[4,2304]{1,0:T(4,128)}, u32[]{:S(2)}) copy-start(f32[4,2304]{1,0:T(4,128)} %param.25) | copy-start | bytes 110596
  79.1 5.4 copy-start.7
  79.1 6.4 copy-start.10
  79.2 5.5 collective-permute-start
  80.5 5.0 collective-permute-start.1
  84.6 1.7 slice-start
  93.2 2.1 copy-start.6
  150.5 1.3 copy-start.4
  151.8 455.8 %all-gather.15.cloned.1.call-start = ((), (), s32[]{:S(2)}) async-start(), calls=%async_computation.2 | async-start | bytes 18874368 | tf_op jit(solution)/shard_map/all_gather | solution.py:34
  181.5 1.4 copy-start.5
  182.9 477.4 %all-gather.13.cloned.1.call-start = ((), (), s32[]{:S(2)}) async-start(), calls=%async_computation.1 | async-start | bytes 5242880 | tf_op jit(solution)/shard_map/all_gather | solution.py:50
  381.8 6.0 copy-start.11
  381.8 2.6 copy-start.3
  384.8 2.6 copy-start.3
  624.6 2.6 copy-start.2
  627.7 2.6 copy-start.2
  630.7 2.5 copy-start.8
  655.1 5.2 copy-start.12
  660.3 11.6 %copy-start.1 = (bf16[1024,32]{0,1:T(8,128)(2,1)S(1)}, bf16[1024,32]{0,1:T(8,128)(2,1)}, u32[]{:S(2)}) copy-start(bf16[1024,32]{0,1:T(8,128)(2,1)} %param.24) | copy-start | bytes 196612
Sparse Core Ops, SparseCore 0:
  8.9 61.6 all-gather.10
  151.9 227.6 all-gather.16
  381.8 225.7 all-gather.14
  609.0 34.7 all-gather.12
where the time goes:
time: 686 us; the launch traced here: 678 us
  waiting for transfers between devices  384 us (56%)
  local copies, waits for them, and re-layouts  159 us (23%)
  matrix products  47.8 us (7%)
  other arithmetic  39.5 us (6%)
  blocking collectives  28.1 us (4%)
  between operations  13.6 us (2%)
    all_gather x2, waiting for transfers between devices, entering(): gathered = jax.tree.map(lambda a: lax.all_gather(a, axis), part)  324 us
    all_gather x2, waiting for transfers between devices, contract_rows(): lax.all_gather(weight, 'batch', axis=0, tiled=True)  58.1 us
    slice x3, local copies, waits for them, and re-layouts, span_parts(): values = act[:, :, :INNER].reshape(groups, span_count, SPAN, HEADS, HEADDIM)  35.6 us
    reshape x4, local copies, waits for them, and re-layouts, finish(): return result.reshape(groups, span_count * SPAN, INNER)  34.2 us
    rev x1, local copies, waits for them, and re-layouts, on_device(): backward_y = jnp.flip(finish(behind_parts, behind_in[1], d_skip), 1)  32.6 us
    all_gather x2, blocking collectives, entering(): gathered = jax.tree.map(lambda a: lax.all_gather(a, axis), part)  28.1 us
    reshape x4, local copies, waits for them, and re-layouts, span_parts(): values = act[:, :, :INNER].reshape(groups, span_count, SPAN, HEADS, HEADDIM)  27.5 us
    dot_general x2, matrix products, contract_rows(): jnp.einsum('gtd,dk->gtk', activations, lax.all_gather(weight, 'batch', ax...  17.2 us
  transfers between devices with their start and end apart: 6, of which 4 were waited for; matrix products, arithmetic and copies ran while one was open for 23% of the time, Pallas kernels for 0%

commit v1 on v0

v1 whole, which is shorter than its diff:
```python
import jax
import jax.numpy as jnp
from jax import lax
from jax.experimental import pallas as pl
from jax.experimental.pallas import tpu as pltpu
from jax.sharding import PartitionSpec as P

INNER = 2048
HEADS = 32
STATE = 128
SPAN = 128
HEADDIM = 64
PAIRS = INNER // 128
CONVW = INNER + 2 * STATE
F32 = jnp.float32
BF16 = jnp.bfloat16
BIG = pltpu.CompilerParams(vmem_limit_bytes=48 * 1024 * 1024)


def cost(flops, moved, exps):
    return pl.CostEstimate(flops=int(flops), bytes_accessed=int(moved), transcendentals=int(exps))


def silu(x):
    return x / (1.0 + jnp.exp(-x))


def spread(cells, pair):
    rows = cells.shape[0]
    low = jnp.broadcast_to(cells[:, 2 * pair : 2 * pair + 1], (rows, 128))
    high = jnp.broadcast_to(cells[:, 2 * pair + 1 : 2 * pair + 2], (rows, 128))
    return jnp.where(lax.broadcasted_iota(jnp.int32, (rows, 128), 1) < HEADDIM, low, high)


def states_kernel(
    conv, before, after, weight, bias, scaled_f, scaled_b, growth_f, growth_b,
    act_f, act_b, states_f, states_b, total_f, total_b, pad,
):
    length = conv.shape[0]
    spans = length // SPAN

    @pl.loop(0, CONVW // 128)
    def _(j):
        cols = pl.ds(pl.multiple_of(j * 128, 128), 128)
        pad[0:8, :] = before[:, cols].astype(F32)
        pad[8 : 8 + length, :] = conv[:, cols].astype(F32)
        pad[8 + length : 16 + length, :] = after[:, cols].astype(F32)
        taps = [weight[k : k + 1, cols] for k in range(4)]
        start = bias[:, cols]
        for k in range(spans):
            base = k * SPAN + 5
            ahead = start
            behind = start
            for tap in range(4):
                ahead = ahead + taps[tap] * pad[base + tap : base + tap + SPAN, :]
                behind = behind + taps[tap] * pad[base + 6 - tap : base + 6 - tap + SPAN, :]
            act_f[k * SPAN : (k + 1) * SPAN, cols] = silu(ahead).astype(BF16)
            act_b[k * SPAN : (k + 1) * SPAN, cols] = silu(behind).astype(BF16)

    for act, scaled, growth, states, total, order in (
        (act_f, scaled_f, growth_f, states_f, total_f, range(spans)),
        (act_b, scaled_b, growth_b, states_b, total_b, range(spans - 1, -1, -1)),
    ):

        @pl.loop(0, spans)
        def _(k):
            rows = pl.ds(pl.multiple_of(k * SPAN, SPAN), SPAN)
            write = act[rows, INNER : INNER + STATE].astype(F32).T.astype(BF16)
            scale = scaled[rows, :]
            for group in range(PAIRS // 2):
                parts = []
                for pair in (2 * group, 2 * group + 1):
                    vals = act[rows, pair * 128 : (pair + 1) * 128].astype(F32)
                    parts.append((vals * spread(scale, pair)).astype(BF16))
                states[rows, group * 256 : (group + 1) * 256] = jnp.dot(
                    write, jnp.concatenate(parts, 1), preferred_element_type=F32
                )

        for pair in range(PAIRS):
            cols = slice(pair * 128, (pair + 1) * 128)
            running = None
            for k in order:
                fresh = states[k * SPAN : (k + 1) * SPAN, cols]
                running = fresh if running is None else growth[k : k + 1, cols] * running + fresh
            total[:, cols] = running


def within_kernel(act_f, act_b, cum_f, cum_b, row_f, row_b, row_dt, skip, y_f, y_b):
    down = lax.broadcasted_iota(jnp.int32, (SPAN, SPAN), 0)
    across = lax.broadcasted_iota(jnp.int32, (SPAN, SPAN), 1)
    low_lanes = across < HEADDIM
    for act, cum, row, out, causal in (
        (act_f, cum_f, row_f, y_f, down >= across),
        (act_b, cum_b, row_b, y_b, down <= across),
    ):
        write = act[:, INNER : INNER + STATE]
        read = act[:, INNER + STATE :]
        scores = lax.dot_general(
            read, write, (((1,), (1,)), ((), ())), preferred_element_type=F32
        )
        column = cum[...]
        for pair in range(PAIRS):
            mixes = []
            for head in (2 * pair, 2 * pair + 1):
                gap = column[:, head : head + 1] - row[head : head + 1, :]
                decay = jnp.exp(jnp.where(causal, gap, -jnp.inf))
                mixes.append((scores * decay * row_dt[head : head + 1, :]).astype(BF16))
            cols = slice(pair * 128, (pair + 1) * 128)
            vals = act[:, cols]
            wide = vals.astype(F32)
            apart = jnp.concatenate(
                [
                    jnp.where(low_lanes, wide, 0.0).astype(BF16),
                    jnp.where(low_lanes, 0.0, wide).astype(BF16),
                ],
                0,
            )
            inner = jnp.dot(jnp.concatenate(mixes, 1), apart, preferred_element_type=F32)
            out[:, cols] = inner + skip[:, cols] * wide


def finish_kernel(
    y_f, y_b, gate, read_f, read_b, cum_f, cum_b, states_f, states_b, in_f, in_b,
    growth_f, growth_b, gain, weight, turn, out, entry_f, entry_b, gated_f, gated_b, comb,
):
    step = pl.program_id(0)
    spans = entry_f.shape[0] // SPAN

    @pl.when(step == 0)
    def _():
        for states, start, growth, entry, order in (
            (states_f, in_f, growth_f, entry_f, range(spans)),
            (states_b, in_b, growth_b, entry_b, range(spans - 1, -1, -1)),
        ):
            for pair in range(PAIRS):
                cols = slice(pair * 128, (pair + 1) * 128)
                running = start[:, cols].astype(F32)
                for k in order:
                    rows = slice(k * SPAN, (k + 1) * SPAN)
                    entry[rows, cols] = running.astype(BF16)
                    running = growth[k : k + 1, cols] * running + states[rows, cols]

    rows = pl.ds(pl.multiple_of(step * SPAN, SPAN), SPAN)
    scales = []
    grown_f, grown_b = jnp.exp(cum_f[...]), jnp.exp(cum_b[...])
    square_f = jnp.zeros((SPAN, 128), F32)
    square_b = jnp.zeros((SPAN, 128), F32)
    for group in range(PAIRS // 2):
        wide = slice(group * 256, (group + 1) * 256)
        from_f = jnp.dot(read_f[...], entry_f[rows, wide], preferred_element_type=F32)
        from_b = jnp.dot(read_b[...], entry_b[rows, wide], preferred_element_type=F32)
        for half in range(2):
            pair = 2 * group + half
            cols = slice(pair * 128, (pair + 1) * 128)
            part = slice(half * 128, (half + 1) * 128)
            opened = silu(gate[:, cols].astype(F32))
            v_f = (y_f[:, cols] + from_f[:, part] * spread(grown_f, pair)) * opened
            v_b = (y_b[:, cols] + from_b[:, part] * spread(grown_b, pair)) * opened
            gated_f[:, cols] = v_f
            gated_b[:, cols] = v_b
            square_f += v_f * v_f
            square_b += v_b * v_b
    scale_f = lax.rsqrt(jnp.sum(square_f, 1, keepdims=True) / INNER + 1e-5)
    scale_b = lax.rsqrt(jnp.sum(square_b, 1, keepdims=True) / INNER + 1e-5)
    for pair in range(PAIRS):
        cols = slice(pair * 128, (pair + 1) * 128)
        both = gated_f[:, cols] * scale_f + gated_b[:, cols] * scale_b
        comb[:, cols] = (both * gain[:, cols]).astype(BF16)
    stream = jnp.dot(comb[...], weight[...], preferred_element_type=F32).astype(BF16)
    out[...] = jnp.dot(stream, turn[...], preferred_element_type=F32).astype(BF16)


def whole(*shape):
    return pl.BlockSpec(shape, lambda *_: (0,) * len(shape))


def on_device(
    hidden, in_weight, dt_weight, conv_weight, conv_bias, dt_bias, a_log, d_skip, norm_gain,
    out_weight,
):
    model = hidden.shape[2] // 2
    half = hidden.shape[1]
    length = 2 * half
    spans = length // SPAN
    count = lax.axis_size("seq")
    odd = lax.axis_index("seq") % 2 == 1
    swap = [(i, i ^ 1) for i in range(count)]
    up = [(i, i + 2) for i in range(count - 2)]
    down = [(i + 2, i) for i in range(count - 2)]

    weight = lax.all_gather(in_weight, "batch", axis=0, tiled=True)
    last_weight = lax.all_gather(out_weight, "batch", axis=0, tiled=True)

    ahead_half, reverse_half = hidden[0, :, :model], hidden[0, :, model:]
    kept = jnp.where(odd, reverse_half, ahead_half)
    got = lax.ppermute(jnp.where(odd, ahead_half, reverse_half), "seq", swap)
    rows = jnp.concatenate([jnp.where(odd, got, kept), jnp.where(odd, kept, got)], 0)
    a = lax.broadcasted_iota(jnp.int32, (model, model), 0)
    b = lax.broadcasted_iota(jnp.int32, (model, model), 1)
    turn = jnp.where(odd, a + b == model - 1, a == b).astype(BF16)
    stream = jnp.dot(rows, turn, preferred_element_type=F32).astype(BF16)

    step = jax.nn.softplus(
        jnp.dot(stream, dt_weight, preferred_element_type=F32) + dt_bias[None]
    )
    rates = (step * -jnp.exp(a_log)[None]).reshape(spans, SPAN, HEADS)
    place = jnp.arange(SPAN)
    lower = (place[:, None] >= place[None]).astype(F32)
    high = lax.Precision.HIGHEST
    cum_f = jnp.einsum("ts,ksh->kth", lower, rates, precision=high)
    cum_b = jnp.einsum("ts,ksh->kth", lower.T, rates, precision=high)
    end_f, end_b = cum_f[:, -1], cum_b[:, 0]
    step_spans = step.reshape(spans, SPAN, HEADS)
    scaled_f = (jnp.exp(end_f[:, None] - cum_f) * step_spans).reshape(length, HEADS)
    scaled_b = (jnp.exp(end_b[:, None] - cum_b) * step_spans).reshape(length, HEADS)
    growth_f = jnp.repeat(jnp.exp(end_f), HEADDIM, 1)
    growth_b = jnp.repeat(jnp.exp(end_b), HEADDIM, 1)
    cum_f, cum_b = cum_f.reshape(length, HEADS), cum_b.reshape(length, HEADS)
    row_f, row_b, row_dt = cum_f.T, cum_b.T, step.T

    projected = jnp.dot(stream, weight, preferred_element_type=F32).astype(BF16)
    conv_in = projected[:, INNER:]
    before = lax.ppermute(conv_in[-8:], "seq", up)
    after = lax.ppermute(conv_in[:8], "seq", down)

    like = jax.ShapeDtypeStruct
    act_f, act_b, states_f, states_b, total_f, total_b = pl.pallas_call(
        states_kernel,
        out_shape=[like((length, CONVW), BF16)] * 2
        + [like((length, INNER), F32)] * 2
        + [like((STATE, INNER), F32)] * 2,
        scratch_shapes=[pltpu.VMEM((length + 16, 128), F32)],
        compiler_params=BIG,
        cost_estimate=cost(8e9, 20e6, 3e6),
        name="states",
    )(
        conv_in, before, after, conv_weight, conv_bias[None], scaled_f, scaled_b, growth_f,
        growth_b,
    )

    def entering(total, growth, moves):
        decay = jnp.prod(growth, 0)[None]
        state = jnp.zeros((STATE, INNER), BF16)
        for lap in range(count // 2 - 1):
            outgoing = total if lap == 0 else total + decay * state.astype(F32)
            state = lax.ppermute(outgoing.astype(BF16), "seq", moves)
        return state

    in_f = entering(total_f, growth_f, up)
    in_b = entering(total_b, growth_b, down)

    def strip(width, at=0):
        return pl.BlockSpec((SPAN, width), lambda k: (k, at))

    def slab():
        return pl.BlockSpec((HEADS, SPAN), lambda k: (0, k))

    y_f, y_b = pl.pallas_call(
        within_kernel,
        grid=(spans,),
        in_specs=[strip(CONVW)] * 2 + [strip(HEADS)] * 2 + [slab()] * 3 + [whole(1, INNER)],
        out_specs=[strip(INNER)] * 2,
        out_shape=[like((length, INNER), F32)] * 2,
        compiler_params=BIG,
        cost_estimate=cost(25e9, 15e6, 5e6),
        name="within",
    )(act_f, act_b, cum_f, cum_b, row_f, row_b, row_dt, jnp.repeat(d_skip, HEADDIM)[None])

    out = pl.pallas_call(
        finish_kernel,
        grid=(spans,),
        in_specs=[strip(INNER)] * 2
        + [strip(INNER)]
        + [strip(STATE, CONVW // STATE - 1)] * 2
        + [strip(HEADS)] * 2
        + [whole(length, INNER)] * 2
        + [whole(STATE, INNER)] * 2
        + [whole(spans, INNER)] * 2
        + [whole(1, INNER), whole(INNER, model), whole(model, model)],
        out_specs=strip(model),
        out_shape=like((length, model), BF16),
        scratch_shapes=[pltpu.VMEM((length, INNER), BF16)] * 2
        + [pltpu.VMEM((SPAN, INNER), F32)] * 2
        + [pltpu.VMEM((SPAN, INNER), BF16)],
        compiler_params=BIG,
        cost_estimate=cost(8e9, 20e6, 2e6),
        name="finish",
    )(
        y_f, y_b, projected, act_f, act_b, cum_f, cum_b, states_f, states_b, in_f, in_b,
        growth_f, growth_b, norm_gain[None], last_weight, turn,
    )

    first, second = out[:half], out[half:]
    mine = jnp.where(odd, second, first)
    back = lax.ppermute(jnp.where(odd, first, second), "seq", swap)
    return jnp.concatenate([jnp.where(odd, back, mine), jnp.where(odd, mine, back)], 1)[None]


def solution(mesh):
    placed = (
        P("batch", "seq", None), P("batch", None), P(), P(), P(), P(), P(), P(), P(),
        P("batch", None),
    )
    return jax.shard_map(
        on_device, mesh=mesh, in_specs=placed, out_specs=P("batch", "seq", None), check_vma=False
    )
```

time: 686 us -> 203 us (0.30)
  the two profiles are of different devices: /device:TPU:31 before, /device:TPU:0 now
where the time goes in v1:
time: 203 us; the launch traced here: 202 us
  waiting for transfers between devices  82.4 us (41%)
  Pallas kernels  43.3 us (21%)
  starting transfers between devices  30.2 us (15%)
  between operations  13.7 us (7%)
  matrix products  12 us (6%)
  other arithmetic  11.5 us (6%)
  local copies, waits for them, and re-layouts  8.9 us (4%)
    all_gather x1, waiting for transfers between devices, on_device(): weight = lax.all_gather(in_weight, 'batch', axis=0, tiled=True)  46.8 us
    ppermute x6, starting transfers between devices, entering(): state = lax.ppermute(outgoing.astype(BF16), 'seq', moves)  19.8 us
    pallas_call x1, Pallas kernels, on_device(): pl.pallas_call(finish_kernel, grid=(spans,), in_specs=[strip(INNER)] * 2...  17.9 us
    pallas_call x1, Pallas kernels, on_device(): pl.pallas_call(states_kernel, out_shape=[like((length, CONVW), BF16)] * 2...  17.5 us
    ppermute x6, waiting for transfers between devices, entering(): state = lax.ppermute(outgoing.astype(BF16), 'seq', moves)  13.3 us
    ppermute x1, waiting for transfers between devices, on_device(): got = lax.ppermute(jnp.where(odd, ahead_half, reverse_half), 'seq', swap)  11.8 us
    dot_general x1, matrix products, on_device(): projected = jnp.dot(stream, weight, preferred_element_type=F32).astype(BF16)  9.95 us
    ppermute x1, waiting for transfers between devices, on_device(): back = lax.ppermute(jnp.where(odd, first, second), 'seq', swap)  9.75 us
  transfers between devices with their start and end apart: 12, of which 6 were waited for; matrix products, arithmetic and copies ran while one was open for 14% of the time, Pallas kernels for 13%

profile of v1, /device:TPU:0, one launch (start us, length us, event | category | flops | bytes accessed | tf_op | source)
XLA Modules:
  0.0 202.1 jit_solution(135914634107914320)
XLA Ops:
  8.6 3.0 %collective-permute-start = (bf16[256,1024]{1,0:T(8,128)(2,1)S(1)}, bf16[256,1024]{1,0:T(8,128)(2,1)S(1)}, u32[]{:S(2)}, u32[]{:S(2)}) collective-permute-start(bf16[256,1024]{1,0:T(8,128)(2,1)S(1)} %select_bitcast_fusion), channel_id=1, source_target_pairs={{0,4},{4,0},{8,12},{12,8},{16,20},{20,16},{24,28},{28,24},{1,5},{5... | collective-permute-start | bytes 1572872 | tf_op jit(solution)/shard_map/ppermute | solution.py:196
  11.7 11.8 %collective-permute-done = bf16[256,1024]{1,0:T(8,128)(2,1)S(1)} collective-permute-done((bf16[256,1024]{1,0:T(8,128)(2,1)S(1)}, bf16[256,1024]{1,0:T(8,128)(2,1)S(1)}, u32[]{:S(2)}, u32[]{:S(2)}) %collective-permute-start) | collective-permute-done | bytes 524320 | tf_op jit(solution)/shard_map/ppermute | solution.py:196
  26.2 46.8 %all-gather.3.cloned.1.call-done = bf16[1024,4352]{1,0:T(8,128)(2,1)} async-done(((bf16[256,4352]{1,0:T(8,128)(2,1)}), bf16[1024,4352]{1,0:T(8,128)(2,1)}) %all-gather.3.cloned.1.call-update) | async-done | bytes 8912912 | tf_op jit(solution)/shard_map/all_gather | solution.py:191
  72.9 10.0 %convolution_convert_fusion.gate = bf16[512,4352]{1,0:T(8,128)(2,1)} fusion(bf16[512,1024]{1,0:T(8,128)(2,1)S(1)} %fusion.6, bf16[1024,4352]{1,0:T(8,128)(2,1)} %all-gather.3.cloned.1.call-done), kind=kOutput, calls=%fused_computation | convolution fusion | flops 4565630976 | bytes 14417920 | tf_op jit(solution)/shard_map/dot_general | solution.py:221
  83.7 1.3 collective-permute-start.2
  85.0 4.5 %collective-permute-start.1 = (bf16[8,2304]{1,0:T(8,128)(2,1)S(1)}, bf16[8,2304]{1,0:T(8,128)(2,1)S(1)}, u32[]{:S(2)}, u32[]{:S(2)}) collective-permute-start(bf16[8,2304]{1,0:T(8,128)(2,1)S(1)} %get-tuple-element.22), channel_id=1, source_target_pairs={{0,8},{4,12},{8,16},{12,20},{16,24},{20,28},{1,9},{5,13},{9,17},{1... | collective-permute-start | bytes 110600 | tf_op jit(solution)/shard_map/ppermute | solution.py:223
  90.2 3.2 %slice.38.conv = bf16[512,2304]{1,0:T(8,128)(2,1)} slice(bf16[512,4352]{1,0:T(8,128)(2,1)} %convolution_convert_fusion.gate), slice={[0:512], [2048:4352]} | slice | bytes 4718592 | tf_op jit(solution)/shard_map/slice | solution.py:222
  93.4 17.5 %states.1 = (bf16[512,2304]{1,0:T(8,128)(2,1)S(1)}, bf16[512,2304]{1,0:T(8,128)(2,1)}, f32[512,2048]{1,0:T(8,128)}, f32[512,2048]{1,0:T(8,128)}, f32[128,2048]{1,0:T(8,128)S(1)}, /*index=5*/f32[128,2048]{1,0:T(8,128)S(1)}) custom-call(bf16[512,2304]{1,0:T(8,128)(2,1)} %slice.38.conv, bf16[8,2304]{1,0:T(8,128)(2,1)S(1)} %collective-permute-done.1.before, ...), custom_call_target="tpu_custom_call" | custom-call | flops 8000000000 | bytes 20000000 | tf_op jit(solution)/shard_map/states/pallas_call | solution.py:227
  111.0 1.5 copy-done.2
  112.5 1.3 collective-permute-start.6
  113.9 5.4 %collective-permute-start.3 = (bf16[128,2048]{1,0:T(8,128)(2,1)S(1)}, bf16[128,2048]{1,0:T(8,128)(2,1)}, u32[]{:S(2)}, u32[]{:S(2)}) collective-permute-start(bf16[128,2048]{1,0:T(8,128)(2,1)S(1)} %convert_element_type.42), channel_id=1, source_target_pairs={{0,8},{4,12},{8,16},{12,20},{16,24},{20,28},{1,9},{5,13},{9,17},{1... | collective-permute-start | bytes 1572872 | tf_op jit(solution)/shard_map/ppermute | solution.py:246
  119.6 8.5 %collective-permute-done.6 = bf16[128,2048]{1,0:T(8,128)(2,1)} collective-permute-done((bf16[128,2048]{1,0:T(8,128)(2,1)S(1)}, bf16[128,2048]{1,0:T(8,128)(2,1)}, u32[]{:S(2)}, u32[]{:S(2)}) %collective-permute-start.6) | collective-permute-done | bytes 524320 | tf_op jit(solution)/shard_map/ppermute | solution.py:246
  128.1 2.0 %add_convert_fusion.1 = bf16[128,2048]{1,0:T(8,128)(2,1)} fusion(f32[128,2048]{1,0:T(8,128)S(1)} %get-tuple-element.20, bf16[128,2048]{1,0:T(8,128)(2,1)} %collective-permute-done.6, f32[2048]{0:T(1024)S(1)} %mul.54), kind=kLoop, calls=%fused_computation.17 | loop fusion | flops 1048576 | bytes 2105344 | tf_op jit(solution)/shard_map/convert_element_type | solution.py:246
  131.4 2.0 add_convert_fusion.3
  133.4 5.4 %collective-permute-start.4 = (bf16[128,2048]{1,0:T(8,128)(2,1)}, bf16[128,2048]{1,0:T(8,128)(2,1)}, u32[]{:S(2)}, u32[]{:S(2)}) collective-permute-start(bf16[128,2048]{1,0:T(8,128)(2,1)} %add_convert_fusion.3), channel_id=1, source_target_pairs={{0,8},{4,12},{8,16},{12,20},{16,24},{20,28},{1,9},{5,13},{9,17},{1... | collective-permute-start | bytes 1572872 | tf_op jit(solution)/shard_map/ppermute | solution.py:246
  138.8 1.7 fusion.1.turn
  141.1 3.8 %collective-permute-done.7 = bf16[128,2048]{1,0:T(8,128)(2,1)S(1)} collective-permute-done((bf16[128,2048]{1,0:T(8,128)(2,1)}, bf16[128,2048]{1,0:T(8,128)(2,1)S(1)}, u32[]{:S(2)}, u32[]{:S(2)}) %collective-permute-start.7) | collective-permute-done | bytes 524320 | tf_op jit(solution)/shard_map/ppermute | solution.py:246
  148.1 2.0 add_convert_fusion.2
  150.1 5.3 %collective-permute-start.5 = (bf16[128,2048]{1,0:T(8,128)(2,1)}, bf16[128,2048]{1,0:T(8,128)(2,1)}, u32[]{:S(2)}, u32[]{:S(2)}) collective-permute-start(bf16[128,2048]{1,0:T(8,128)(2,1)} %add_convert_fusion.2), channel_id=1, source_target_pairs={{0,8},{4,12},{8,16},{12,20},{16,24},{20,28},{1,9},{5,13},{9,17},{1... | collective-permute-start | bytes 1572872 | tf_op jit(solution)/shard_map/ppermute | solution.py:246
  155.4 1.7 copy-done.4
  157.0 7.8 %within.1 = (f32[512,2048]{1,0:T(8,128)}, f32[512,2048]{1,0:T(8,128)}) custom-call(bf16[512,2304]{1,0:T(8,128)(2,1)S(1)} %copy-done.3, bf16[512,2304]{1,0:T(8,128)(2,1)S(1)} %copy-done.4, f32[512,32]{1,0:T(8,128)S(1)} %bitcast.57, f32[512,32]{1,0:T(8,128)S(1)} %bitcast.60, f32[32,512]{1,0:T(8,128)S(1)} %copy.29.row_f, f32[32,512]{1,0:T(8,128)S(1)} %copy.30.row_b, ...), custom_call_target="tpu_custom_call" | custom-call | flops 24999999488 | bytes 15000000 | tf_op jit(solution)/shard_map/within/pallas_call | solution.py:258
  164.8 17.9 %finish.1 = bf16[512,1024]{1,0:T(8,128)(2,1)S(1)} custom-call(f32[512,2048]{1,0:T(8,128)} %get-tuple-element.15.y_f, f32[512,2048]{1,0:T(8,128)} %get-tuple-element.16.y_b, bf16[512,4352]{1,0:T(8,128)(2,1)} %convolution_convert_fusion.gate, bf16[512,2304]{1,0:T(8,128)(2,1)} %copy-done.2, bf16[512,2304]{1,0:T(8,128)(2,1)} %get-tuple-element.14.act_b.read_b, ...), custom_call_target="tpu_custom_call" | custom-call | flops 8000000000 | bytes 20000000 | tf_op jit(solution)/shard_map/finish/pallas_call | solution.py:269
  182.8 1.5 collective-permute-start.9
  184.3 9.8 %collective-permute-done.9 = bf16[256,1024]{1,0:T(8,128)(2,1)S(1)} collective-permute-done((bf16[256,1024]{1,0:T(8,128)(2,1)S(1)}, bf16[256,1024]{1,0:T(8,128)(2,1)S(1)}, u32[]{:S(2)}, u32[]{:S(2)}) %collective-permute-start.9) | collective-permute-done | bytes 524320 | tf_op jit(solution)/shard_map/ppermute | solution.py:295
  (71 shorter events, 12.9 us)
Async XLA Ops:
  6.5 18.3 %copy-start = (bf16[1024,32]{0,1:T(8,128)(2,1)S(1)}, bf16[1024,32]{0,1:T(8,128)(2,1)}, u32[]{:S(2)}) copy-start(bf16[1024,32]{0,1:T(8,128)(2,1)} %param.12) | copy-start | bytes 196612
  6.5 17.0 %copy-start.7 = (bf16[1,256,2048]{2,1,0:T(8,128)(2,1)S(1)}, bf16[1,256,2048]{2,1,0:T(8,128)(2,1)}, u32[]{:S(2)}) copy-start(bf16[1,256,2048]{2,1,0:T(8,128)(2,1)} %param.10) | copy-start | bytes 3145732
  6.5 5.1 %copy-start.8 = (f32[2304]{0:T(1024)S(1)}, f32[2304]{0:T(1024)}, u32[]{:S(2)}) copy-start(f32[2304]{0:T(1024)} %param.14) | copy-start | bytes 27652
  6.5 5.1 %copy-start.11 = (f32[32]{0:T(128)S(1)}, f32[32]{0:T(128)}, u32[]{:S(2)}) copy-start(f32[32]{0:T(128)} %param.16) | copy-start | bytes 388
  6.5 66.4 %all-gather.3.cloned.1.call-start = ((), (), s32[]{:S(2)}) async-start(), calls=%async_computation | async-start | bytes 11141120 | tf_op jit(solution)/shard_map/all_gather | solution.py:191
  7.3 157.5 %all-gather.5.cloned.1.call-start = ((), (), s32[]{:S(2)}) async-start(), calls=%async_computation.1 | async-start | bytes 5242880 | tf_op jit(solution)/shard_map/all_gather | solution.py:192
  8.6 14.9 %collective-permute-start = (bf16[256,1024]{1,0:T(8,128)(2,1)S(1)}, bf16[256,1024]{1,0:T(8,128)(2,1)S(1)}, u32[]{:S(2)}, u32[]{:S(2)}) collective-permute-start(bf16[256,1024]{1,0:T(8,128)(2,1)S(1)} %select_bitcast_fusion), channel_id=1, source_target_pairs={{0,4},{4,0},{8,12},{12,8},{16,20},{20,16},{24,28},{28,24},{1,5},{5... | collective-permute-start | bytes 1572872 | tf_op jit(solution)/shard_map/ppermute | solution.py:196
  23.6 1.3 copy-start.9
  82.9 10.6 %copy-start.6 = (f32[4,2304]{1,0:T(4,128)S(1)}, f32[4,2304]{1,0:T(4,128)}, u32[]{:S(2)}) copy-start(f32[4,2304]{1,0:T(4,128)} %weight.1) | copy-start | bytes 110596
  83.7 9.7 %collective-permute-start.2 = (bf16[8,2304]{1,0:T(8,128)(2,1)S(1)}, bf16[8,2304]{1,0:T(8,128)(2,1)S(1)}, u32[]{:S(2)}, u32[]{:S(2)}) collective-permute-start(bf16[8,2304]{1,0:T(8,128)(2,1)S(1)} %get-tuple-element.21), channel_id=1, source_target_pairs={{8,0},{12,4},{16,8},{20,12},{24,16},{28,20},{9,1},{13,5},{17,9},{2... | collective-permute-start | bytes 110600 | tf_op jit(solution)/shard_map/ppermute | solution.py:224
  85.0 8.4 %collective-permute-start.1 = (bf16[8,2304]{1,0:T(8,128)(2,1)S(1)}, bf16[8,2304]{1,0:T(8,128)(2,1)S(1)}, u32[]{:S(2)}, u32[]{:S(2)}) collective-permute-start(bf16[8,2304]{1,0:T(8,128)(2,1)S(1)} %get-tuple-element.22), channel_id=1, source_target_pairs={{0,8},{4,12},{8,16},{12,20},{16,24},{20,28},{1,9},{5,13},{9,17},{1... | collective-permute-start | bytes 110600 | tf_op jit(solution)/shard_map/ppermute | solution.py:223
  111.0 1.5 copy-start.2
  112.5 27.9 %copy-start.10 = (f32[32]{0:T(128)S(1)}, f32[32]{0:T(128)}, u32[]{:S(2)}) copy-start(f32[32]{0:T(128)} %param.17) | copy-start | bytes 388
  112.5 15.5 %collective-permute-start.6 = (bf16[128,2048]{1,0:T(8,128)(2,1)S(1)}, bf16[128,2048]{1,0:T(8,128)(2,1)}, u32[]{:S(2)}, u32[]{:S(2)}) collective-permute-start(bf16[128,2048]{1,0:T(8,128)(2,1)S(1)} %convert_element_type.47), channel_id=1, source_target_pairs={{8,0},{12,4},{16,8},{20,12},{24,16},{28,20},{9,1},{13,5},{17,9},{2... | collective-permute-start | bytes 1572872 | tf_op jit(solution)/shard_map/ppermute | solution.py:246
  113.9 17.5 %collective-permute-start.3 = (bf16[128,2048]{1,0:T(8,128)(2,1)S(1)}, bf16[128,2048]{1,0:T(8,128)(2,1)}, u32[]{:S(2)}, u32[]{:S(2)}) collective-permute-start(bf16[128,2048]{1,0:T(8,128)(2,1)S(1)} %convert_element_type.42), channel_id=1, source_target_pairs={{0,8},{4,12},{8,16},{12,20},{16,24},{20,28},{1,9},{5,13},{9,17},{1... | collective-permute-start | bytes 1572872 | tf_op jit(solution)/shard_map/ppermute | solution.py:246
  130.1 14.7 %collective-permute-start.7 = (bf16[128,2048]{1,0:T(8,128)(2,1)}, bf16[128,2048]{1,0:T(8,128)(2,1)S(1)}, u32[]{:S(2)}, u32[]{:S(2)}) collective-permute-start(bf16[128,2048]{1,0:T(8,128)(2,1)} %add_convert_fusion.1), channel_id=1, source_target_pairs={{8,0},{12,4},{16,8},{20,12},{24,16},{28,20},{9,1},{13,5},{17,9},{2... | collective-permute-start | bytes 1572872 | tf_op jit(solution)/shard_map/ppermute | solution.py:246
  133.4 14.7 %collective-permute-start.4 = (bf16[128,2048]{1,0:T(8,128)(2,1)}, bf16[128,2048]{1,0:T(8,128)(2,1)}, u32[]{:S(2)}, u32[]{:S(2)}) collective-permute-start(bf16[128,2048]{1,0:T(8,128)(2,1)} %add_convert_fusion.3), channel_id=1, source_target_pairs={{0,8},{4,12},{8,16},{12,20},{16,24},{20,28},{1,9},{5,13},{9,17},{1... | collective-permute-start | bytes 1572872 | tf_op jit(solution)/shard_map/ppermute | solution.py:246
  141.1 14.3 %copy-start.3 = (bf16[512,2304]{1,0:T(8,128)(2,1)S(1)}, bf16[512,2304]{1,0:T(8,128)(2,1)}, u32[]{:S(2)}) copy-start(bf16[512,2304]{1,0:T(8,128)(2,1)} %copy-done.2) | copy-start | bytes 7077892
  145.8 19.0 %collective-permute-start.8 = (bf16[128,2048]{1,0:T(8,128)(2,1)}, bf16[128,2048]{1,0:T(8,128)(2,1)S(1)}, u32[]{:S(2)}, u32[]{:S(2)}) collective-permute-start(bf16[128,2048]{1,0:T(8,128)(2,1)} %add_convert_fusion), channel_id=1, source_target_pairs={{8,0},{12,4},{16,8},{20,12},{24,16},{28,20},{9,1},{13,5},{17,9},{2... | collective-permute-start | bytes 1572872 | tf_op jit(solution)/shard_map/ppermute | solution.py:246
  150.1 14.7 %collective-permute-start.5 = (bf16[128,2048]{1,0:T(8,128)(2,1)}, bf16[128,2048]{1,0:T(8,128)(2,1)}, u32[]{:S(2)}, u32[]{:S(2)}) collective-permute-start(bf16[128,2048]{1,0:T(8,128)(2,1)} %add_convert_fusion.2), channel_id=1, source_target_pairs={{0,8},{4,12},{8,16},{12,20},{16,24},{20,28},{1,9},{5,13},{9,17},{1... | collective-permute-start | bytes 1572872 | tf_op jit(solution)/shard_map/ppermute | solution.py:246
  155.4 1.7 copy-start.4
  157.0 7.8 %copy-start.1 = (bf16[1024,1024]{1,0:T(8,128)(2,1)S(1)}, bf16[1024,1024]{1,0:T(8,128)(2,1)}, u32[]{:S(2)}) copy-start(bf16[1024,1024]{1,0:T(8,128)(2,1)} %fusion.1.turn) | copy-start | bytes 6291460
  157.0 7.8 %copy-start.5 = (f32[2048]{0:T(1024)S(1)}, f32[2048]{0:T(1024)}, u32[]{:S(2)}) copy-start(f32[2048]{0:T(1024)} %param.18) | copy-start | bytes 24580
  182.8 11.2 %collective-permute-start.9 = (bf16[256,1024]{1,0:T(8,128)(2,1)S(1)}, bf16[256,1024]{1,0:T(8,128)(2,1)S(1)}, u32[]{:S(2)}, u32[]{:S(2)}) collective-permute-start(bf16[256,1024]{1,0:T(8,128)(2,1)S(1)} %broadcast_select_fusion.4), channel_id=1, source_target_pairs={{0,4},{4,0},{8,12},{12,8},{16,20},{20,16},{24,28},{28,24},{1,5},{5... | collective-permute-start | bytes 1572872 | tf_op jit(solution)/shard_map/ppermute | solution.py:295
Sparse Core Ops, SparseCore 0:
  8.9 63.9 all-gather.2
  74.5 34.4 all-gather.4

commit v2 on v1

--- a/solution.py
+++ b/solution.py
@@ -12,6 +12,10 @@
 HEADDIM = 64
 PAIRS = INNER // 128
 CONVW = INNER + 2 * STATE
+EDGE = 16
+CHUNKS = 8
+PIECES = 4
+MESH = pl.DeviceIdType.MESH
 F32 = jnp.float32
 BF16 = jnp.bfloat16
 BIG = pltpu.CompilerParams(vmem_limit_bytes=48 * 1024 * 1024)
@@ -33,22 +37,23 @@
 
 
 def states_kernel(
-    conv, before, after, weight, bias, scaled_f, scaled_b, growth_f, growth_b,
+    proj, weight, bias, scaled_f, scaled_b, growth_f, growth_b,
     act_f, act_b, states_f, states_b, total_f, total_b, pad,
 ):
-    length = conv.shape[0]
+    length = act_f.shape[0]
     spans = length // SPAN
 
     @pl.loop(0, CONVW // 128)
     def _(j):
         cols = pl.ds(pl.multiple_of(j * 128, 128), 128)
-        pad[0:8, :] = before[:, cols].astype(F32)
-        pad[8 : 8 + length, :] = conv[:, cols].astype(F32)
-        pad[8 + length : 16 + length, :] = after[:, cols].astype(F32)
+        source = pl.ds(pl.multiple_of(INNER + j * 128, 128), 128)
+        pad[0:EDGE, :] = proj[length : length + EDGE, source].astype(F32)
+        pad[EDGE : EDGE + length, :] = proj[0:length, source].astype(F32)
+        pad[EDGE + length :, :] = proj[length + EDGE :, source].astype(F32)
         taps = [weight[k : k + 1, cols] for k in range(4)]
         start = bias[:, cols]
         for k in range(spans):
-            base = k * SPAN + 5
+            base = k * SPAN + EDGE - 3
             ahead = start
             behind = start
             for tap in range(4):
@@ -170,6 +175,207 @@
     out[...] = jnp.dot(stream, turn[...], preferred_element_type=F32).astype(BF16)
 
 
+def collect_kernel(hidden, shard, rows, weight, blank, local, swap, halo, ysem, zsem, csem, osem):
+    place, part = lax.axis_index("seq"), lax.axis_index("batch")
+    count = lax.axis_size("seq")
+    odd = place % 2
+    upper = (place // 2) % 2
+    half, model = hidden.shape[1], hidden.shape[2] // 2
+    depth = shard.shape[0]
+    piece = depth // 2 // CHUNKS
+    beside = (place + 1 - 2 * odd, part)
+    along = (place + 2 - 4 * upper, part)
+    across = (place, (part + 2) % 4)
+    core = (place, part + 1 - 2 * (part % 2))
+    slant = place - 1 + 2 * odd
+
+    barrier = pltpu.get_barrier_semaphore()
+
+    def greet(device):
+        pl.semaphore_signal(barrier, inc=1, device_id=device, device_id_type=MESH)
+
+    for device in (beside, across, core):
+        greet(device)
+    lower_there, upper_there = place >= 2, place + 2 < count
+    slant_there = (slant >= 0) & (slant < count)
+
+    for there, seat in ((lower_there, place - 2), (upper_there, place + 2), (slant_there, slant)):
+
+        @pl.when(there)
+        def _(seat=seat):
+            greet((seat, part))
+
+    others = [there.astype(jnp.int32) for there in (lower_there, upper_there, slant_there)]
+    pl.semaphore_wait(barrier, 3 + sum(others))
+
+    def remote(src, dst, sems, at, device):
+        return pltpu.make_async_remote_copy(
+            src_ref=src, dst_ref=dst, send_sem=sems.at[0, at], recv_sem=sems.at[1, at],
+            device_id=device, device_id_type=MESH,
+        )
+
+    def mine(i, side):
+        return shard.at[pl.ds(pl.multiple_of(side * (depth // 2) + i * piece, 16), piece)]
+
+    def slot(owner, i, side):
+        at = owner * depth + side * (depth // 2) + i * piece
+        return weight.at[pl.ds(pl.multiple_of(at, 16), piece)]
+
+    def whole_slot(owner):
+        return weight.at[pl.ds(pl.multiple_of(owner * depth, 16), depth)]
+
+    far = (part + 2) % 4
+    over_y = [remote(mine(i, upper), slot(part, i, upper), ysem, i, across) for i in range(CHUNKS)]
+    for copy in over_y:
+        copy.start()
+    spot = rows.at[pl.ds(pl.multiple_of(odd * half, 16), half)]
+    kept_cols = pl.ds(pl.multiple_of(odd * model, 128), model)
+    sent_cols = pl.ds(pl.multiple_of((1 - odd) * model, 128), model)
+    swapping = remote(hidden.at[0, :, sent_cols], spot, swap, 0, beside)
+    swapping.start()
+    own_core = remote(shard, whole_slot(part), osem, 0, core)
+    own_core.start()
+    own = pltpu.make_async_copy(shard, whole_slot(part), local.at[0])
+    own.start()
+    kept = pltpu.make_async_copy(hidden.at[0, :, kept_cols], spot, local.at[1])
+    kept.start()
+
+    before = rows.at[pl.ds(2 * half, EDGE)]
+    after = rows.at[pl.ds(2 * half + EDGE, EDGE)]
+    last, first = pl.ds(half - EDGE, EDGE), pl.ds(0, EDGE)
+    low_cols, high_cols = pl.ds(0, model), pl.ds(model, model)
+    halos = [
+        ((odd == 1) & upper_there, hidden.at[0, last, high_cols], before, 0, place + 2),
+        ((odd == 1) & slant_there, hidden.at[0, last, low_cols], before, 0, place + 1),
+        ((odd == 0) & lower_there, hidden.at[0, first, low_cols], after, 1, place - 2),
+        ((odd == 0) & slant_there, hidden.at[0, first, high_cols], after, 1, place - 1),
+    ]
+
+    def halo_copy(at):
+        there, src, dst, kind, seat = halos[at]
+        return there, pltpu.make_async_remote_copy(
+            src_ref=src, dst_ref=dst, send_sem=halo.at[0, at], recv_sem=halo.at[1, kind],
+            device_id=(seat, part), device_id_type=MESH,
+        )
+
+    for at in range(4):
+        there, copy = halo_copy(at)
+
+        @pl.when(there)
+        def _(copy=copy):
+            copy.start()
+
+    blank[...] = jnp.zeros_like(blank)
+    pair_last = count // 2 - 1
+    for missing, dst, at in ((place // 2 == 0, before, 2), (place // 2 == pair_last, after, 3)):
+
+        @pl.when(missing)
+        def _(dst=dst, at=at):
+            fill = pltpu.make_async_copy(blank, dst, local.at[at])
+            fill.start()
+            fill.wait()
+
+    on_z = [remote(slot(far, i, upper), slot(far, i, upper), zsem, i, along) for i in range(CHUNKS)]
+    first_core = [
+        remote(slot(far, i, upper), slot(far, i, upper), csem, i, core) for i in range(CHUNKS)
+    ]
+    from_z = [
+        remote(slot(far, i, 1 - upper), slot(far, i, 1 - upper), zsem, i, along)
+        for i in range(CHUNKS)
+    ]
+    second_core = [
+        remote(slot(far, i, 1 - upper), slot(far, i, 1 - upper), csem, CHUNKS + i, core)
+        for i in range(CHUNKS)
+    ]
+    for i in range(CHUNKS + 1):
+        if i < CHUNKS:
+            over_y[i].wait_recv()
+            on_z[i].start()
+            first_core[i].start()
+        if i > 0:
+            from_z[i - 1].wait_recv()
+            second_core[i - 1].start()
+    for i in range(CHUNKS):
+        over_y[i].wait_send()
+        on_z[i].wait_send()
+        first_core[i].wait()
+        second_core[i].wait()
+    own.wait()
+    kept.wait()
+    own_core.wait()
+    swapping.wait()
+    for at in range(4):
+        there, copy = halo_copy(at)
+
+        @pl.when(there)
+        def _(copy=copy):
+            copy.wait_send()
+
+    for there, dst, kind in ((place // 2 > 0, before, 0), (place // 2 < pair_last, after, 1)):
+
+        @pl.when(there)
+        def _(dst=dst, kind=kind):
+            pltpu.make_async_remote_copy(
+                src_ref=dst, dst_ref=dst, send_sem=halo.at[0, kind], recv_sem=halo.at[1, kind],
+                device_id=beside, device_id_type=MESH,
+            ).wait_recv()
+
+
+def chain_kernel(total_f, total_b, decay_f, decay_b, in_f, in_b, out_f, out_b, land_f, land_b, fsem, bsem):
+    place, part = lax.axis_index("seq"), lax.axis_index("batch")
+    count = lax.axis_size("seq")
+    lower_there, upper_there = place >= 2, place + 2 < count
+    barrier = pltpu.get_barrier_semaphore()
+    for there, seat in ((lower_there, place - 2), (upper_there, place + 2)):
+
+        @pl.when(there)
+        def _(seat=seat):
+            pl.semaphore_signal(barrier, inc=1, device_id=(seat, part), device_id_type=MESH)
+
+    pl.semaphore_wait(barrier, lower_there.astype(jnp.int32) + upper_there.astype(jnp.int32))
+
+    width = total_f.shape[1] // PIECES
+    ways = (
+        (total_f, decay_f, in_f, out_f, land_f, fsem, lower_there, upper_there, place + 2),
+        (total_b, decay_b, in_b, out_b, land_b, bsem, upper_there, lower_there, place - 2),
+    )
+
+    def hop(way, piece):
+        _, _, _, out, land, sems, _, _, seat = way
+        return pltpu.make_async_remote_copy(
+            src_ref=out.at[piece], dst_ref=land.at[piece], send_sem=sems.at[0, piece],
+            recv_sem=sems.at[1, piece], device_id=(seat, part), device_id_type=MESH,
+        )
+
+    for piece in range(PIECES):
+        cols = slice(piece * width, (piece + 1) * width)
+        for way in ways:
+            total, decay, entry, out, land, sems, source, target, seat = way
+
+            @pl.when(source)
+            def _():
+                hop(way, piece).wait_recv()
+                state = land[piece]
+                entry[:, cols] = state
+                out[piece] = (total[:, cols] + decay[:, cols] * state.astype(F32)).astype(BF16)
+
+            @pl.when(jnp.logical_not(source))
+            def _():
+                entry[:, cols] = jnp.zeros((STATE, width), BF16)
+                out[piece] = total[:, cols].astype(BF16)
+
+            @pl.when(target)
+            def _():
+                hop(way, piece).start()
+
+    for piece in range(PIECES):
+        for way in ways:
+
+            @pl.when(way[7])
+            def _():
+                hop(way, piece).wait_send()
+
+
 def whole(*shape):
     return pl.BlockSpec(shape, lambda *_: (0,) * len(shape))
 
@@ -185,23 +391,36 @@
     count = lax.axis_size("seq")
     odd = lax.axis_index("seq") % 2 == 1
     swap = [(i, i ^ 1) for i in range(count)]
-    up = [(i, i + 2) for i in range(count - 2)]
-    down = [(i + 2, i) for i in range(count - 2)]
-
-    weight = lax.all_gather(in_weight, "batch", axis=0, tiled=True)
+
+    like = jax.ShapeDtypeStruct
+    anywhere = pl.BlockSpec(memory_space=pl.ANY)
+    dma = pltpu.SemaphoreType.DMA
+    rows, weight = pl.pallas_call(
+        collect_kernel,
+        in_specs=[anywhere] * 2,
+        out_specs=[anywhere] * 2,
+        out_shape=[
+            like((length + 2 * EDGE, model), BF16),
+            like((4 * in_weight.shape[0], in_weight.shape[1]), BF16),
+        ],
+        scratch_shapes=[
+            pltpu.VMEM((EDGE, model), BF16), dma((4,)), dma((2, 1)), dma((2, 4)),
+            dma((2, CHUNKS)), dma((2, CHUNKS)), dma((2, 2 * CHUNKS)), dma((2, 1)),
+        ],
+        compiler_params=pltpu.CompilerParams(collective_id=0, has_side_effects=True),
+        cost_estimate=cost(0, 20e6, 0),
+        name="collect",
+    )(hidden, in_weight)
+    out_weight, weight = lax.optimization_barrier((out_weight, weight))
     last_weight = lax.all_gather(out_weight, "batch", axis=0, tiled=True)
 
-    ahead_half, reverse_half = hidden[0, :, :model], hidden[0, :, model:]
-    kept = jnp.where(odd, reverse_half, ahead_half)
-    got = lax.ppermute(jnp.where(odd, ahead_half, reverse_half), "seq", swap)
-    rows = jnp.concatenate([jnp.where(odd, got, kept), jnp.where(odd, kept, got)], 0)
     a = lax.broadcasted_iota(jnp.int32, (model, model), 0)
     b = lax.broadcasted_iota(jnp.int32, (model, model), 1)
     turn = jnp.where(odd, a + b == model - 1, a == b).astype(BF16)
     stream = jnp.dot(rows, turn, preferred_element_type=F32).astype(BF16)
 
     step = jax.nn.softplus(
-        jnp.dot(stream, dt_weight, preferred_element_type=F32) + dt_bias[None]
+        jnp.dot(stream[:length], dt_weight, preferred_element_type=F32) + dt_bias[None]
     )
     rates = (step * -jnp.exp(a_log)[None]).reshape(spans, SPAN, HEADS)
     place = jnp.arange(SPAN)
@@ -219,35 +438,30 @@
     row_f, row_b, row_dt = cum_f.T, cum_b.T, step.T
 
     projected = jnp.dot(stream, weight, preferred_element_type=F32).astype(BF16)
-    conv_in = projected[:, INNER:]
-    before = lax.ppermute(conv_in[-8:], "seq", up)
-    after = lax.ppermute(conv_in[:8], "seq", down)
-
-    like = jax.ShapeDtypeStruct
     act_f, act_b, states_f, states_b, total_f, total_b = pl.pallas_call(
         states_kernel,
         out_shape=[like((length, CONVW), BF16)] * 2
         + [like((length, INNER), F32)] * 2
         + [like((STATE, INNER), F32)] * 2,
-        scratch_shapes=[pltpu.VMEM((length + 16, 128), F32)],
+        scratch_shapes=[pltpu.VMEM((length + 2 * EDGE, 128), F32)],
         compiler_params=BIG,
         cost_estimate=cost(8e9, 20e6, 3e6),
         name="states",
     )(
-        conv_in, before, after, conv_weight, conv_bias[None], scaled_f, scaled_b, growth_f,
-        growth_b,
+        projected, conv_weight, conv_bias[None], scaled_f, scaled_b, growth_f, growth_b,
     )
 
-    def entering(total, growth, moves):
-        decay = jnp.prod(growth, 0)[None]
-        state = jnp.zeros((STATE, INNER), BF16)
-        for lap in range(count // 2 - 1):
-            outgoing = total if lap == 0 else total + decay * state.astype(F32)
-            state = lax.ppermute(outgoing.astype(BF16), "seq", moves)
-        return state
-
-    in_f = entering(total_f, growth_f, up)
-    in_b = entering(total_b, growth_b, down)
+    in_f, in_b = pl.pallas_call(
+        chain_kernel,
+        out_shape=[like((STATE, INNER), BF16)] * 2,
+        scratch_shapes=[pltpu.VMEM((PIECES, STATE, INNER // PIECES), BF16)] * 4
+        + [dma((2, PIECES))] * 2,
+        compiler_params=pltpu.CompilerParams(
+            collective_id=1, has_side_effects=True, vmem_limit_bytes=32 * 1024 * 1024
+        ),
+        cost_estimate=cost(2e6, 8e6, 0),
+        name="chain",
+    )(total_f, total_b, jnp.prod(growth_f, 0)[None], jnp.prod(growth_b, 0)[None])
 
     def strip(width, at=0):
         return pl.BlockSpec((SPAN, width), lambda k: (k, at))

time: 203 us -> 274 us (1.35)
  Pallas kernels: 43.3 us -> 230 us
  waiting for transfers between devices: 82.4 us -> 7.69 us
  starting transfers between devices: 30.2 us -> 1.57 us
  other arithmetic: 11.5 us -> 1.76 us
  local copies, waits for them, and re-layouts: 8.9 us -> 3.61 us
    pallas_call x0 -> x2, Pallas kernels: none -> 187 us  [the longest x1 98.5 us: on_device(): pl.pallas_call(chain_kernel, out_shape=[like((STATE, INNER), BF16)] * 2,...]
    all_gather x1 -> x0, waiting for transfers between devices: 46.8 us -> none  [on_device(): weight = lax.all_gather(in_weight, 'batch', axis=0, tiled=True)]
    ppermute x9 -> x0, starting transfers between devices: 28.7 us -> none  [the longest x6 19.8 us: entering(): state = lax.ppermute(outgoing.astype(BF16), 'seq', moves)]
    ppermute x9 -> x0, waiting for transfers between devices: 25.2 us -> none  [the longest x6 13.3 us: entering(): state = lax.ppermute(outgoing.astype(BF16), 'seq', moves)]
    convert_element_type x6 -> x0, other arithmetic: 7.07 us -> none  [entering(): state = lax.ppermute(outgoing.astype(BF16), 'seq', moves)]
    slice x2 -> x0, local copies, waits for them, and re-layouts: 4.05 us -> none  [the longest x1 3.21 us: on_device(): conv_in = projected[:, INNER:]]
  transfers between devices with their start and end apart: 12 -> 2, of which waited for: 6 -> 1; matrix products, arithmetic and copies ran while one was open for 14% -> 6% of each run, Pallas kernels for 13% -> 46%
where the time goes in v2:
time: 274 us; the launch traced here: 273 us
  Pallas kernels  230 us (84%)
  matrix products  14.7 us (5%)
  between operations  13.6 us (5%)
  waiting for transfers between devices  7.69 us (3%)
  local copies, waits for them, and re-layouts  3.61 us (1%)
    pallas_call x1, Pallas kernels, on_device(): pl.pallas_call(chain_kernel, out_shape=[like((STATE, INNER), BF16)] * 2,...  98.5 us
    pallas_call x1, Pallas kernels, on_device(): pl.pallas_call(collect_kernel, in_specs=[anywhere] * 2, out_specs=[anywhe...  88.2 us
    pallas_call x1, Pallas kernels, on_device(): pl.pallas_call(states_kernel, out_shape=[like((length, CONVW), BF16)] * 2...  18.1 us
    pallas_call x1, Pallas kernels, on_device(): pl.pallas_call(finish_kernel, grid=(spans,), in_specs=[strip(INNER)] * 2...  17.6 us
    dot_general x1, matrix products, on_device(): projected = jnp.dot(stream, weight, preferred_element_type=F32).astype(BF16)  11.3 us
    pallas_call x1, Pallas kernels, on_device(): pl.pallas_call(within_kernel, grid=(spans,), in_specs=[strip(CONVW)] * 2...  8.01 us
    ppermute x1, waiting for transfers between devices, on_device(): back = lax.ppermute(jnp.where(odd, first, second), 'seq', swap)  7.67 us
  transfers between devices with their start and end apart: 2, of which 1 were waited for; matrix products, arithmetic and copies ran while one was open for 6% of the time, Pallas kernels for 46%

profile of v2, /device:TPU:0, one launch (start us, length us, event | category | flops | bytes accessed | tf_op | source)
XLA Modules:
  0.0 273.4 jit_solution(13611375767067692422)
XLA Ops:
  6.5 88.2 %collect.1 = (bf16[544,1024]{1,0:T(8,128)(2,1)}, bf16[1024,4352]{1,0:T(8,128)(2,1)}) custom-call(bf16[1,256,2048]{2,1,0:T(8,128)(2,1)} %hidden.1, bf16[256,4352]{1,0:T(8,128)(2,1)} %shard.1), custom_call_target="tpu_custom_call" | custom-call | bytes 20000000 | tf_op jit(solution)/shard_map/collect/pallas_call | solution.py:398
  94.9 2.6 fusion.6
  97.5 0.5 compare_select_fusion
  98.2 0.2 convolution_bitcast_fusion.1
  98.4 0.1 copy.27
  98.6 0.2 convolution_bitcast_fusion
  98.8 0.1 copy.28
  98.9 0.2 slice_reduce_fusion
  99.8 0.1 copy.29.row_f
  99.9 0.1 copy.30.row_b
  100.0 0.1 bitcast_multiply_fusion
  100.1 0.1 copy.26
  100.3 0.1 copy.23
  100.4 11.3 %convolution_convert_fusion.proj.gate = bf16[544,4352]{1,0:T(8,128)(2,1)} fusion(bf16[544,1024]{1,0:T(8,128)(2,1)S(1)} %fusion.6, bf16[1024,4352]{1,0:T(8,128)(2,1)} %get-tuple-element.21), kind=kOutput, calls=%fused_computation | convolution fusion | flops 4850982912 | bytes 14761984 | tf_op jit(solution)/shard_map/dot_general | solution.py:440
  111.7 18.1 %states.1 = (bf16[512,2304]{1,0:T(8,128)(2,1)S(1)}, bf16[512,2304]{1,0:T(8,128)(2,1)}, f32[512,2048]{1,0:T(8,128)}, f32[512,2048]{1,0:T(8,128)}, f32[128,2048]{1,0:T(8,128)S(1)}, /*index=5*/f32[128,2048]{1,0:T(8,128)S(1)}) custom-call(bf16[544,4352]{1,0:T(8,128)(2,1)} %convolution_convert_fusion.proj.gate, f32[4,2304]{1,0:T(4,128)S(1)} %copy-done.6, ...), custom_call_target="tpu_custom_call" | custom-call | flops 8000000000 | bytes 20000000 | tf_op jit(solution)/shard_map/states/pallas_call | solution.py:441
  129.8 98.5 %chain.1 = (bf16[128,2048]{1,0:T(8,128)(2,1)S(1)}, bf16[128,2048]{1,0:T(8,128)(2,1)S(1)}) custom-call(f32[128,2048]{1,0:T(8,128)S(1)} %get-tuple-element.28.total_f, f32[128,2048]{1,0:T(8,128)S(1)} %get-tuple-element.29.total_b, f32[1,2048]{1,0:T(1,128)S(1)} %broadcast_in_dim.32.decay_f, f32[1,2048]{1,0:T(1,128)S(1)} %broadcast_in_dim.33.decay_b), custom_call_target="tpu_custom_call" | custom-call | flops 2000000 | bytes 8000000 | tf_op jit(solution)/shard_map/chain/pallas_call | solution.py:454
  228.3 0.8 copy-done.3
  229.1 0.3 fusion.1.turn
  229.4 8.0 %within.1 = (f32[512,2048]{1,0:T(8,128)}, f32[512,2048]{1,0:T(8,128)}) custom-call(bf16[512,2304]{1,0:T(8,128)(2,1)S(1)} %get-tuple-element.22.act_f.read_f, bf16[512,2304]{1,0:T(8,128)(2,1)S(1)} %copy-done.2, f32[512,32]{1,0:T(8,128)S(1)} %bitcast.52, f32[512,32]{1,0:T(8,128)S(1)} %bitcast.55, f32[32,512]{1,0:T(8,128)S(1)} %copy.29.row_f, ...), custom_call_target="tpu_custom_call" | custom-call | flops 24999999488 | bytes 15000000 | tf_op jit(solution)/shard_map/within/pallas_call | solution.py:472
  237.5 1.0 copy-done.4
  238.5 17.6 %finish.1 = bf16[512,1024]{1,0:T(8,128)(2,1)S(1)} custom-call(f32[512,2048]{1,0:T(8,128)} %get-tuple-element.24.y_f, f32[512,2048]{1,0:T(8,128)} %get-tuple-element.25.y_b, bf16[544,4352]{1,0:T(8,128)(2,1)} %convolution_convert_fusion.proj.gate, bf16[512,2304]{1,0:T(8,128)(2,1)} %copy-done.1, bf16[512,2304]{1,0:T(8,128)(2,1)} %get-tuple-element.23.act_b.read_b, ...), custom_call_target="tpu_custom_call" | custom-call | flops 8000000000 | bytes 20000000 | tf_op jit(solution)/shard_map/finish/pallas_call | solution.py:483
  256.1 1.6 collective-permute-start
  257.7 7.7 %collective-permute-done = bf16[256,1024]{1,0:T(8,128)(2,1)S(1)} collective-permute-done((bf16[256,1024]{1,0:T(8,128)(2,1)S(1)}, bf16[256,1024]{1,0:T(8,128)(2,1)S(1)}, u32[]{:S(2)}, u32[]{:S(2)}) %collective-permute-start) | collective-permute-done | bytes 524320 | tf_op jit(solution)/shard_map/ppermute | solution.py:509
  265.5 1.0 maximum_bitcast_fusion
  (40 shorter events, 1.2 us)
Async XLA Ops:
  6.5 90.9 %copy-start = (bf16[1024,32]{0,1:T(8,128)(2,1)S(1)}, bf16[1024,32]{0,1:T(8,128)(2,1)}, u32[]{:S(2)}) copy-start(bf16[1024,32]{0,1:T(8,128)(2,1)} %param.12) | copy-start | bytes 196612
  6.5 230.9 %all-gather.2.cloned.1.call-start = ((), (), s32[]{:S(2)}) async-start(), calls=%async_computation | async-start | bytes 5242880 | tf_op jit(solution)/shard_map/all_gather | solution.py:415
  94.8 2.6 copy-start.9
  94.8 3.1 %copy-start.10 = (f32[32]{0:T(128)S(1)}, f32[32]{0:T(128)}, u32[]{:S(2)}) copy-start(f32[32]{0:T(128)} %param.16) | copy-start | bytes 388
  94.8 3.1 %copy-start.7 = (f32[2304]{0:T(1024)S(1)}, f32[2304]{0:T(1024)}, u32[]{:S(2)}) copy-start(f32[2304]{0:T(1024)} %param.14) | copy-start | bytes 27652
  94.9 3.1 %copy-start.8 = (f32[32]{0:T(128)S(1)}, f32[32]{0:T(128)}, u32[]{:S(2)}) copy-start(f32[32]{0:T(128)} %param.17) | copy-start | bytes 388
  100.4 11.3 %copy-start.6 = (f32[4,2304]{1,0:T(4,128)S(1)}, f32[4,2304]{1,0:T(4,128)}, u32[]{:S(2)}) copy-start(f32[4,2304]{1,0:T(4,128)} %weight.1) | copy-start | bytes 110596
  129.8 99.6 %copy-start.1 = (bf16[512,2304]{1,0:T(8,128)(2,1)}, bf16[512,2304]{1,0:T(8,128)(2,1)S(1)}, u32[]{:S(2)}) copy-start(bf16[512,2304]{1,0:T(8,128)(2,1)S(1)} %get-tuple-element.22.act_f.read_f) | copy-start | bytes 7077892
  129.8 99.6 %copy-start.2 = (bf16[512,2304]{1,0:T(8,128)(2,1)S(1)}, bf16[512,2304]{1,0:T(8,128)(2,1)}, u32[]{:S(2)}) copy-start(bf16[512,2304]{1,0:T(8,128)(2,1)} %get-tuple-element.23.act_b.read_b) | copy-start | bytes 7077892
  228.3 0.8 copy-start.3
  229.4 8.0 %copy-start.5 = (f32[2048]{0:T(1024)S(1)}, f32[2048]{0:T(1024)}, u32[]{:S(2)}) copy-start(f32[2048]{0:T(1024)} %param.18) | copy-start | bytes 24580
  237.4 1.0 copy-start.4
  256.1 9.2 %collective-permute-start = (bf16[256,1024]{1,0:T(8,128)(2,1)S(1)}, bf16[256,1024]{1,0:T(8,128)(2,1)S(1)}, u32[]{:S(2)}, u32[]{:S(2)}) collective-permute-start(bf16[256,1024]{1,0:T(8,128)(2,1)S(1)} %broadcast_select_fusion.3), channel_id=1, source_target_pairs={{0,4},{4,0},{8,12},{12,8},{16,20},{20,16},{24,28},{28,24},{1,5},{5... | collective-permute-start | bytes 1572872 | tf_op jit(solution)/shard_map/ppermute | solution.py:509
Sparse Core Ops, SparseCore 0:
  94.9 34.7 all-gather.1

commit v3 on v1

--- a/solution.py
+++ b/solution.py
@@ -12,6 +12,9 @@
 HEADDIM = 64
 PAIRS = INNER // 128
 CONVW = INNER + 2 * STATE
+EDGE = 16
+PIECES = 4
+MESH = pl.DeviceIdType.MESH
 F32 = jnp.float32
 BF16 = jnp.bfloat16
 BIG = pltpu.CompilerParams(vmem_limit_bytes=48 * 1024 * 1024)
@@ -33,22 +36,23 @@
 
 
 def states_kernel(
-    conv, before, after, weight, bias, scaled_f, scaled_b, growth_f, growth_b,
+    proj, weight, bias, scaled_f, scaled_b, growth_f, growth_b,
     act_f, act_b, states_f, states_b, total_f, total_b, pad,
 ):
-    length = conv.shape[0]
+    length = act_f.shape[0]
     spans = length // SPAN
 
     @pl.loop(0, CONVW // 128)
     def _(j):
         cols = pl.ds(pl.multiple_of(j * 128, 128), 128)
-        pad[0:8, :] = before[:, cols].astype(F32)
-        pad[8 : 8 + length, :] = conv[:, cols].astype(F32)
-        pad[8 + length : 16 + length, :] = after[:, cols].astype(F32)
+        source = pl.ds(pl.multiple_of(INNER + j * 128, 128), 128)
+        pad[0:EDGE, :] = proj[length : length + EDGE, source].astype(F32)
+        pad[EDGE : EDGE + length, :] = proj[0:length, source].astype(F32)
+        pad[EDGE + length :, :] = proj[length + EDGE :, source].astype(F32)
         taps = [weight[k : k + 1, cols] for k in range(4)]
         start = bias[:, cols]
         for k in range(spans):
-            base = k * SPAN + 5
+            base = k * SPAN + EDGE - 3
             ahead = start
             behind = start
             for tap in range(4):
@@ -170,6 +174,79 @@
     out[...] = jnp.dot(stream, turn[...], preferred_element_type=F32).astype(BF16)
 
 
+def chain_kernel(total_f, total_b, decay_f, decay_b, in_f, in_b, out_f, out_b, land_f, land_b, fsem, bsem):
+    place, part = lax.axis_index("seq"), lax.axis_index("batch")
+    count = lax.axis_size("seq")
+    lower_there, upper_there = place >= 2, place + 2 < count
+    barrier = pltpu.get_barrier_semaphore()
+    for there, seat in ((lower_there, place - 2), (upper_there, place + 2)):
+
+        @pl.when(there)
+        def _(seat=seat):
+            pl.semaphore_signal(barrier, inc=1, device_id=(seat, part), device_id_type=MESH)
+
+    pl.semaphore_wait(barrier, lower_there.astype(jnp.int32) + upper_there.astype(jnp.int32))
+
+    width = total_f.shape[1] // PIECES
+    ways = (
+        (total_f, decay_f, in_f, out_f, land_f, fsem, lower_there, upper_there, place + 2),
+        (total_b, decay_b, in_b, out_b, land_b, bsem, upper_there, lower_there, place - 2),
+    )
+
+    def hop(way, piece):
+        _, _, _, out, land, sems, _, _, seat = way
+        return pltpu.make_async_remote_copy(
+            src_ref=out.at[piece], dst_ref=land.at[piece], send_sem=sems.at[0, piece],
+            recv_sem=sems.at[1, piece], device_id=(seat, part), device_id_type=MESH,
+        )
+
+    def begin(way):
+        total, _, entry, out, _, _, source, target, _ = way
+
+        @pl.when(jnp.logical_not(source))
+        def _():
+            for piece in range(PIECES):
+                cols = slice(piece * width, (piece + 1) * width)
+                out[piece] = total[:, cols].astype(BF16)
+                hop(way, piece).start()
+                entry[:, cols] = jnp.zeros((STATE, width), BF16)
+
+    def relay(way, piece):
+        total, decay, entry, out, land, _, source, target, _ = way
+        cols = slice(piece * width, (piece + 1) * width)
+
+        @pl.when(source)
+        def _():
+            hop(way, piece).wait_recv()
+
+            @pl.when(target)
+            def _():
+                passed = decay[:, cols] * land[piece].astype(F32)
+                out[piece] = (total[:, cols] + passed).astype(BF16)
+                hop(way, piece).start()
+
+            entry[:, cols] = land[piece]
+
+    for way in ways:
+        begin(way)
+
+    nearer = place < count // 2
+    for near, order in ((nearer, ways), (jnp.logical_not(nearer), ways[::-1])):
+
+        @pl.when(near)
+        def _(order=order):
+            for piece in range(PIECES):
+                for way in order:
+                    relay(way, piece)
+
+    for piece in range(PIECES):
+        for way in ways:
+
+            @pl.when(way[7])
+            def _():
+                hop(way, piece).wait_send()
+
+
 def whole(*shape):
     return pl.BlockSpec(shape, lambda *_: (0,) * len(shape))
 
@@ -185,23 +262,29 @@
     count = lax.axis_size("seq")
     odd = lax.axis_index("seq") % 2 == 1
     swap = [(i, i ^ 1) for i in range(count)]
+
+    like = jax.ShapeDtypeStruct
+    dma = pltpu.SemaphoreType.DMA
     up = [(i, i + 2) for i in range(count - 2)]
     down = [(i + 2, i) for i in range(count - 2)]
-
     weight = lax.all_gather(in_weight, "batch", axis=0, tiled=True)
     last_weight = lax.all_gather(out_weight, "batch", axis=0, tiled=True)
 
     ahead_half, reverse_half = hidden[0, :, :model], hidden[0, :, model:]
     kept = jnp.where(odd, reverse_half, ahead_half)
     got = lax.ppermute(jnp.where(odd, ahead_half, reverse_half), "seq", swap)
-    rows = jnp.concatenate([jnp.where(odd, got, kept), jnp.where(odd, kept, got)], 0)
+    early, late = jnp.where(odd, got, kept), jnp.where(odd, kept, got)
+    before = lax.ppermute(late[-EDGE:], "seq", up)
+    after = lax.ppermute(early[:EDGE], "seq", down)
+    rows = jnp.concatenate([early, late, before, after], 0)
+
     a = lax.broadcasted_iota(jnp.int32, (model, model), 0)
     b = lax.broadcasted_iota(jnp.int32, (model, model), 1)
     turn = jnp.where(odd, a + b == model - 1, a == b).astype(BF16)
     stream = jnp.dot(rows, turn, preferred_element_type=F32).astype(BF16)
 
     step = jax.nn.softplus(
-        jnp.dot(stream, dt_weight, preferred_element_type=F32) + dt_bias[None]
+        jnp.dot(stream[:length], dt_weight, preferred_element_type=F32) + dt_bias[None]
     )
     rates = (step * -jnp.exp(a_log)[None]).reshape(spans, SPAN, HEADS)
     place = jnp.arange(SPAN)
@@ -219,35 +302,30 @@
     row_f, row_b, row_dt = cum_f.T, cum_b.T, step.T
 
     projected = jnp.dot(stream, weight, preferred_element_type=F32).astype(BF16)
-    conv_in = projected[:, INNER:]
-    before = lax.ppermute(conv_in[-8:], "seq", up)
-    after = lax.ppermute(conv_in[:8], "seq", down)
-
-    like = jax.ShapeDtypeStruct
     act_f, act_b, states_f, states_b, total_f, total_b = pl.pallas_call(
         states_kernel,
         out_shape=[like((length, CONVW), BF16)] * 2
         + [like((length, INNER), F32)] * 2
         + [like((STATE, INNER), F32)] * 2,
-        scratch_shapes=[pltpu.VMEM((length + 16, 128), F32)],
+        scratch_shapes=[pltpu.VMEM((length + 2 * EDGE, 128), F32)],
         compiler_params=BIG,
         cost_estimate=cost(8e9, 20e6, 3e6),
         name="states",
     )(
-        conv_in, before, after, conv_weight, conv_bias[None], scaled_f, scaled_b, growth_f,
-        growth_b,
-    )
-
-    def entering(total, growth, moves):
-        decay = jnp.prod(growth, 0)[None]
-        state = jnp.zeros((STATE, INNER), BF16)
-        for lap in range(count // 2 - 1):
-            outgoing = total if lap == 0 else total + decay * state.astype(F32)
-            state = lax.ppermute(outgoing.astype(BF16), "seq", moves)
-        return state
-
-    in_f = entering(total_f, growth_f, up)
-    in_b = entering(total_b, growth_b, down)
+        projected, conv_weight, conv_bias[None], scaled_f, scaled_b, growth_f, growth_b,
+    )
+
+    in_f, in_b = pl.pallas_call(
+        chain_kernel,
+        out_shape=[like((STATE, INNER), BF16)] * 2,
+        scratch_shapes=[pltpu.VMEM((PIECES, STATE, INNER // PIECES), BF16)] * 4
+        + [dma((2, PIECES))] * 2,
+        compiler_params=pltpu.CompilerParams(
+            collective_id=1, has_side_effects=True, vmem_limit_bytes=32 * 1024 * 1024
+        ),
+        cost_estimate=cost(2e6, 8e6, 0),
+        name="chain",
+    )(total_f, total_b, jnp.prod(growth_f, 0)[None], jnp.prod(growth_b, 0)[None])
 
     def strip(width, at=0):
         return pl.BlockSpec((SPAN, width), lambda k: (k, at))

time: 203 us -> 180 us (0.89)
  Pallas kernels: 43.3 us -> 71.9 us
  waiting for transfers between devices: 82.4 us -> 60 us
  starting transfers between devices: 30.2 us -> 10.4 us
  other arithmetic: 11.5 us -> 2.52 us
    pallas_call x0 -> x1, Pallas kernels: none -> 28.1 us  [on_device(): pl.pallas_call(chain_kernel, out_shape=[like((STATE, INNER), BF16)] * 2,...]
    ppermute x8 -> x2, starting transfers between devices: 25.7 us -> 5.84 us  [the longest x1 4.55 us: on_device(): before = lax.ppermute(late[-EDGE:], 'seq', up)]
    ppermute x8 -> x2, waiting for transfers between devices: 13.3 us -> 1.05 us  [the longest x1 1.04 us: on_device(): before = lax.ppermute(late[-EDGE:], 'seq', up)]
    all_gather x1, waiting for transfers between devices: 46.8 us -> 36.6 us  [on_device(): weight = lax.all_gather(in_weight, 'batch', axis=0, tiled=True)]
    convert_element_type x6 -> x0, other arithmetic: 7.07 us -> none  [entering(): state = lax.ppermute(outgoing.astype(BF16), 'seq', moves)]
    slice x2, local copies, waits for them, and re-layouts: 4.05 us -> 0.01 us  [the longest x1 0.01 us: on_device(): before = lax.ppermute(late[-EDGE:], 'seq', up)]
    unnamed x24 -> x26, local copies, waits for them, and re-layouts: 3.17 us -> 5.96 us
  transfers between devices with their start and end apart: 12 -> 6, of which waited for: 6 -> 4; matrix products, arithmetic and copies ran while one was open for 14% -> 9% of each run, Pallas kernels for 13% -> 30%
where the time goes in v3:
time: 180 us
  Pallas kernels  71.9 us (40%)
  waiting for transfers between devices  60 us (33%)
  between operations  13.7 us (8%)
  matrix products  12.6 us (7%)
  starting transfers between devices  10.4 us (6%)
  local copies, waits for them, and re-layouts  8.53 us (5%)
  other arithmetic  2.52 us (1%)
    all_gather x1, waiting for transfers between devices, on_device(): weight = lax.all_gather(in_weight, 'batch', axis=0, tiled=True)  36.6 us
    pallas_call x1, Pallas kernels, on_device(): pl.pallas_call(chain_kernel, out_shape=[like((STATE, INNER), BF16)] * 2,...  28.1 us
    pallas_call x1, Pallas kernels, on_device(): pl.pallas_call(states_kernel, out_shape=[like((length, CONVW), BF16)] * 2...  18.2 us
    pallas_call x1, Pallas kernels, on_device(): pl.pallas_call(finish_kernel, grid=(spans,), in_specs=[strip(INNER)] * 2...  17.6 us
    ppermute x1, waiting for transfers between devices, on_device(): got = lax.ppermute(jnp.where(odd, ahead_half, reverse_half), 'seq', swap)  11.9 us
    dot_general x1, matrix products, on_device(): projected = jnp.dot(stream, weight, preferred_element_type=F32).astype(BF16)  10.4 us
    ppermute x1, waiting for transfers between devices, on_device(): back = lax.ppermute(jnp.where(odd, first, second), 'seq', swap)  9.7 us
    pallas_call x1, Pallas kernels, on_device(): pl.pallas_call(within_kernel, grid=(spans,), in_specs=[strip(CONVW)] * 2...  7.95 us
  transfers between devices with their start and end apart: 6, of which 4 were waited for; matrix products, arithmetic and copies ran while one was open for 9% of the time, Pallas kernels for 30%

profile of v3, /device:TPU:0, one launch (start us, length us, event | category | flops | bytes accessed | tf_op | source)
XLA Modules:
  0.0 179.6 jit_solution(8255074079111883263)
XLA Ops:
  6.5 0.7 all-gather.3.cloned.1.call-update
  7.3 0.5 copy-done.7
  7.9 3.0 %collective-permute-start = (bf16[256,1024]{1,0:T(8,128)(2,1)S(1)}, bf16[256,1024]{1,0:T(8,128)(2,1)S(1)}, u32[]{:S(2)}, u32[]{:S(2)}) collective-permute-start(bf16[256,1024]{1,0:T(8,128)(2,1)S(1)} %select_bitcast_fusion), channel_id=1, source_target_pairs={{0,4},{4,0},{8,12},{12,8},{16,20},{20,16},{24,28},{28,24},{1,5},{5... | collective-permute-start | bytes 1572872 | tf_op jit(solution)/shard_map/ppermute | solution.py:275
  10.9 11.9 %collective-permute-done = bf16[256,1024]{1,0:T(8,128)(2,1)S(1)} collective-permute-done((bf16[256,1024]{1,0:T(8,128)(2,1)S(1)}, bf16[256,1024]{1,0:T(8,128)(2,1)S(1)}, u32[]{:S(2)}, u32[]{:S(2)}) %collective-permute-start) | collective-permute-done | bytes 524320 | tf_op jit(solution)/shard_map/ppermute | solution.py:275
  22.9 1.3 collective-permute-start.2
  24.2 4.5 %collective-permute-start.1 = (bf16[16,1024]{1,0:T(8,128)(2,1)S(1)}, bf16[16,1024]{1,0:T(8,128)(2,1)S(1)}, u32[]{:S(2)}, u32[]{:S(2)}) collective-permute-start(bf16[16,1024]{1,0:T(8,128)(2,1)S(1)} %slice.36), channel_id=1, source_target_pairs={{0,8},{4,12},{8,16},{12,20},{16,24},{20,28},{1,9},{5,13},{9,17},{1... | collective-permute-start | bytes 98312 | tf_op jit(solution)/shard_map/ppermute | solution.py:277
  29.3 1.0 collective-permute-done.1
  30.3 1.3 fusion.6
  31.7 0.5 compare_select_fusion
  34.4 0.7 bitcast_multiply_fusion
  35.3 1.0 copy.23
  36.3 36.6 %all-gather.3.cloned.1.call-done = bf16[1024,4352]{1,0:T(8,128)(2,1)} async-done(((bf16[256,4352]{1,0:T(8,128)(2,1)}), bf16[1024,4352]{1,0:T(8,128)(2,1)}) %all-gather.3.cloned.1.call-update) | async-done | bytes 8912912 | tf_op jit(solution)/shard_map/all_gather | solution.py:270
  72.9 10.4 %convolution_convert_fusion.proj.gate = bf16[544,4352]{1,0:T(8,128)(2,1)} fusion(bf16[544,1024]{1,0:T(8,128)(2,1)} %copy-done.12, bf16[1024,4352]{1,0:T(8,128)(2,1)} %all-gather.3.cloned.1.call-done), kind=kOutput, calls=%fused_computation | convolution fusion | flops 4850982912 | bytes 14761984 | tf_op jit(solution)/shard_map/dot_general | solution.py:304
  83.4 18.2 %states.1 = (bf16[512,2304]{1,0:T(8,128)(2,1)S(1)}, bf16[512,2304]{1,0:T(8,128)(2,1)}, f32[512,2048]{1,0:T(8,128)}, f32[512,2048]{1,0:T(8,128)}, f32[128,2048]{1,0:T(8,128)S(1)}, /*index=5*/f32[128,2048]{1,0:T(8,128)S(1)}) custom-call(bf16[544,4352]{1,0:T(8,128)(2,1)} %convolution_convert_fusion.proj.gate, f32[4,2304]{1,0:T(4,128)S(1)} %copy-done.6, ...), custom_call_target="tpu_custom_call" | custom-call | flops 8000000000 | bytes 20000000 | tf_op jit(solution)/shard_map/states/pallas_call | solution.py:305
  101.6 28.1 %chain.1 = (bf16[128,2048]{1,0:T(8,128)(2,1)S(1)}, bf16[128,2048]{1,0:T(8,128)(2,1)S(1)}) custom-call(f32[128,2048]{1,0:T(8,128)S(1)} %get-tuple-element.21.total_f, f32[128,2048]{1,0:T(8,128)S(1)} %get-tuple-element.22.total_b, f32[1,2048]{1,0:T(1,128)S(1)} %broadcast_in_dim.32.decay_f, f32[1,2048]{1,0:T(1,128)S(1)} %broadcast_in_dim.33.decay_b), custom_call_target="tpu_custom_call" | custom-call | flops 2000000 | bytes 8000000 | tf_op jit(solution)/shard_map/chain/pallas_call | solution.py:318
  129.8 0.8 copy-done.3
  130.5 1.7 copy-done.2
  132.2 7.9 %within.1 = (f32[512,2048]{1,0:T(8,128)}, f32[512,2048]{1,0:T(8,128)}) custom-call(bf16[512,2304]{1,0:T(8,128)(2,1)S(1)} %get-tuple-element.15.act_f.read_f, bf16[512,2304]{1,0:T(8,128)(2,1)S(1)} %copy-done.2, f32[512,32]{1,0:T(8,128)S(1)} %bitcast.56, f32[512,32]{1,0:T(8,128)S(1)} %bitcast.59, f32[32,512]{1,0:T(8,128)S(1)} %copy.29.row_f, ...), custom_call_target="tpu_custom_call" | custom-call | flops 24999999488 | bytes 15000000 | tf_op jit(solution)/shard_map/within/pallas_call | solution.py:336
  140.2 1.5 copy-done.1
  141.7 1.0 copy-done.4
  142.7 17.6 %finish.1 = bf16[512,1024]{1,0:T(8,128)(2,1)S(1)} custom-call(f32[512,2048]{1,0:T(8,128)} %get-tuple-element.17.y_f, f32[512,2048]{1,0:T(8,128)} %get-tuple-element.18.y_b, bf16[544,4352]{1,0:T(8,128)(2,1)} %convolution_convert_fusion.proj.gate, bf16[512,2304]{1,0:T(8,128)(2,1)} %copy-done.1, bf16[512,2304]{1,0:T(8,128)(2,1)} %get-tuple-element.16.act_b.read_b, ...), custom_call_target="tpu_custom_call" | custom-call | flops 8000000000 | bytes 20000000 | tf_op jit(solution)/shard_map/finish/pallas_call | solution.py:347
  160.4 1.5 collective-permute-start.3
  161.9 9.7 %collective-permute-done.3 = bf16[256,1024]{1,0:T(8,128)(2,1)S(1)} collective-permute-done((bf16[256,1024]{1,0:T(8,128)(2,1)S(1)}, bf16[256,1024]{1,0:T(8,128)(2,1)S(1)}, u32[]{:S(2)}, u32[]{:S(2)}) %collective-permute-start.3) | collective-permute-done | bytes 524320 | tf_op jit(solution)/shard_map/ppermute | solution.py:373
  171.7 1.0 maximum_bitcast_fusion
  (56 shorter events, 3.3 us)
Async XLA Ops:
  6.5 25.1 %copy-start = (bf16[1024,32]{0,1:T(8,128)(2,1)S(1)}, bf16[1024,32]{0,1:T(8,128)(2,1)}, u32[]{:S(2)}) copy-start(bf16[1024,32]{0,1:T(8,128)(2,1)} %param.12) | copy-start | bytes 196612
  6.5 1.3 copy-start.7
  6.5 4.3 %copy-start.10 = (f32[32]{0:T(128)S(1)}, f32[32]{0:T(128)}, u32[]{:S(2)}) copy-start(f32[32]{0:T(128)} %param.16) | copy-start | bytes 388
  6.5 66.4 %all-gather.3.cloned.1.call-start = ((), (), s32[]{:S(2)}) async-start(), calls=%async_computation | async-start | bytes 11141120 | tf_op jit(solution)/shard_map/all_gather | solution.py:270
  7.3 134.4 %all-gather.5.cloned.1.call-start = ((), (), s32[]{:S(2)}) async-start(), calls=%async_computation.1 | async-start | bytes 5242880 | tf_op jit(solution)/shard_map/all_gather | solution.py:271
  7.9 14.9 %collective-permute-start = (bf16[256,1024]{1,0:T(8,128)(2,1)S(1)}, bf16[256,1024]{1,0:T(8,128)(2,1)S(1)}, u32[]{:S(2)}, u32[]{:S(2)}) collective-permute-start(bf16[256,1024]{1,0:T(8,128)(2,1)S(1)} %select_bitcast_fusion), channel_id=1, source_target_pairs={{0,4},{4,0},{8,12},{12,8},{16,20},{20,16},{24,28},{28,24},{1,5},{5... | collective-permute-start | bytes 1572872 | tf_op jit(solution)/shard_map/ppermute | solution.py:275
  10.9 18.2 %copy-start.8 = (f32[2304]{0:T(1024)S(1)}, f32[2304]{0:T(1024)}, u32[]{:S(2)}) copy-start(f32[2304]{0:T(1024)} %param.14) | copy-start | bytes 27652
  10.9 18.2 %copy-start.9 = (f32[32]{0:T(128)S(1)}, f32[32]{0:T(128)}, u32[]{:S(2)}) copy-start(f32[32]{0:T(128)} %param.17) | copy-start | bytes 388
  22.9 6.4 %collective-permute-start.2 = (bf16[16,1024]{1,0:T(8,128)(2,1)S(1)}, bf16[16,1024]{1,0:T(8,128)(2,1)S(1)}, u32[]{:S(2)}, u32[]{:S(2)}) collective-permute-start(bf16[16,1024]{1,0:T(8,128)(2,1)S(1)} %slice.37), channel_id=1, source_target_pairs={{8,0},{12,4},{16,8},{20,12},{24,16},{28,20},{9,1},{13,5},{17,9},{2... | collective-permute-start | bytes 98312 | tf_op jit(solution)/shard_map/ppermute | solution.py:278
  24.2 6.1 %collective-permute-start.1 = (bf16[16,1024]{1,0:T(8,128)(2,1)S(1)}, bf16[16,1024]{1,0:T(8,128)(2,1)S(1)}, u32[]{:S(2)}, u32[]{:S(2)}) collective-permute-start(bf16[16,1024]{1,0:T(8,128)(2,1)S(1)} %slice.36), channel_id=1, source_target_pairs={{0,8},{4,12},{8,16},{12,20},{16,24},{20,28},{1,9},{5,13},{9,17},{1... | collective-permute-start | bytes 98312 | tf_op jit(solution)/shard_map/ppermute | solution.py:277
  29.3 2.4 %copy-start.11 = (f32[32]{0:T(128)S(1)}, f32[32]{0:T(128)}, u32[]{:S(2)}) copy-start(f32[32]{0:T(128)} %param.15) | copy-start | bytes 388
  31.7 1.0 copy-start.12
  36.3 47.1 %copy-start.6 = (f32[4,2304]{1,0:T(4,128)S(1)}, f32[4,2304]{1,0:T(4,128)}, u32[]{:S(2)}) copy-start(f32[4,2304]{1,0:T(4,128)} %weight.1) | copy-start | bytes 110596
  129.7 0.8 copy-start.3
  130.5 1.7 copy-start.2
  132.2 9.5 %copy-start.5 = (f32[2048]{0:T(1024)S(1)}, f32[2048]{0:T(1024)}, u32[]{:S(2)}) copy-start(f32[2048]{0:T(1024)} %param.18) | copy-start | bytes 24580
  140.2 1.5 copy-start.1
  141.7 1.0 copy-start.4
  160.4 11.2 %collective-permute-start.3 = (bf16[256,1024]{1,0:T(8,128)(2,1)S(1)}, bf16[256,1024]{1,0:T(8,128)(2,1)S(1)}, u32[]{:S(2)}, u32[]{:S(2)}) collective-permute-start(bf16[256,1024]{1,0:T(8,128)(2,1)S(1)} %broadcast_select_fusion.4), channel_id=1, source_target_pairs={{0,4},{4,0},{8,12},{12,8},{16,20},{20,16},{24,28},{28,24},{1,5},{5... | collective-permute-start | bytes 1572872 | tf_op jit(solution)/shard_map/ppermute | solution.py:373
Sparse Core Ops, SparseCore 0:
  8.9 63.9 all-gather.2
  74.5 34.4 all-gather.4

commit v4 on v3

--- a/solution.py
+++ b/solution.py
@@ -45,10 +45,9 @@
     @pl.loop(0, CONVW // 128)
     def _(j):
         cols = pl.ds(pl.multiple_of(j * 128, 128), 128)
-        source = pl.ds(pl.multiple_of(INNER + j * 128, 128), 128)
-        pad[0:EDGE, :] = proj[length : length + EDGE, source].astype(F32)
-        pad[EDGE : EDGE + length, :] = proj[0:length, source].astype(F32)
-        pad[EDGE + length :, :] = proj[length + EDGE :, source].astype(F32)
+        pad[0:EDGE, :] = proj[length : length + EDGE, cols].astype(F32)
+        pad[EDGE : EDGE + length, :] = proj[0:length, cols].astype(F32)
+        pad[EDGE + length :, :] = proj[length + EDGE :, cols].astype(F32)
         taps = [weight[k : k + 1, cols] for k in range(4)]
         start = bias[:, cols]
         for k in range(spans):
@@ -267,8 +266,7 @@
     dma = pltpu.SemaphoreType.DMA
     up = [(i, i + 2) for i in range(count - 2)]
     down = [(i + 2, i) for i in range(count - 2)]
-    weight = lax.all_gather(in_weight, "batch", axis=0, tiled=True)
-    last_weight = lax.all_gather(out_weight, "batch", axis=0, tiled=True)
+    weight = lax.all_gather(in_weight[:, INNER:], "batch", axis=0, tiled=True)
 
     ahead_half, reverse_half = hidden[0, :, :model], hidden[0, :, model:]
     kept = jnp.where(odd, reverse_half, ahead_half)
@@ -277,6 +275,8 @@
     before = lax.ppermute(late[-EDGE:], "seq", up)
     after = lax.ppermute(early[:EDGE], "seq", down)
     rows = jnp.concatenate([early, late, before, after], 0)
+    gate_shard, rows = lax.optimization_barrier((in_weight[:, :INNER], rows))
+    gate_weight = lax.all_gather(gate_shard, "batch", axis=0, tiled=True)
 
     a = lax.broadcasted_iota(jnp.int32, (model, model), 0)
     b = lax.broadcasted_iota(jnp.int32, (model, model), 1)
@@ -315,6 +315,8 @@
         projected, conv_weight, conv_bias[None], scaled_f, scaled_b, growth_f, growth_b,
     )
 
+    out_weight, total_f = lax.optimization_barrier((out_weight, total_f))
+    last_weight = lax.all_gather(out_weight, "batch", axis=0, tiled=True)
     in_f, in_b = pl.pallas_call(
         chain_kernel,
         out_shape=[like((STATE, INNER), BF16)] * 2,
@@ -332,6 +334,9 @@
 
     def slab():
         return pl.BlockSpec((HEADS, SPAN), lambda k: (0, k))
+
+    gate_weight, in_f = lax.optimization_barrier((gate_weight, in_f))
+    gate = jnp.dot(stream[:length], gate_weight, preferred_element_type=F32).astype(BF16)
 
     y_f, y_b = pl.pallas_call(
         within_kernel,
@@ -364,7 +369,7 @@
         cost_estimate=cost(8e9, 20e6, 2e6),
         name="finish",
     )(
-        y_f, y_b, projected, act_f, act_b, cum_f, cum_b, states_f, states_b, in_f, in_b,
+        y_f, y_b, gate, act_f, act_b, cum_f, cum_b, states_f, states_b, in_f, in_b,
         growth_f, growth_b, norm_gain[None], last_weight, turn,
     )
 

time: 180 us -> 167 us (0.928)
  waiting for transfers between devices: 60 us -> 33.2 us
  local copies, waits for them, and re-layouts: 8.53 us -> 16.5 us
  matrix products: 12.6 us -> 16.8 us
  other arithmetic: 2.52 us -> 4.35 us
    all_gather x1 -> x2, waiting for transfers between devices: 36.6 us -> 10.5 us  [the longest x1 10.5 us: on_device(): weight = lax.all_gather(in_weight[:, INNER:], 'batch', axis=0, tiled=True)]
    dot_general x0 -> x1, matrix products: none -> 6.46 us  [on_device(): jnp.dot(stream[:length], gate_weight, preferred_element_type=F32)]
    slice x0 -> x2, local copies, waits for them, and re-layouts: none -> 4.79 us  [the longest x1 2.49 us: on_device(): weight = lax.all_gather(in_weight[:, INNER:], 'batch', axis=0, tiled=True)]
    dot_general x1, matrix products: 10.4 us -> 6.3 us  [on_device(): projected = jnp.dot(stream, weight, preferred_element_type=F32).astype(BF16)]
    unnamed x26 -> x44, local copies, waits for them, and re-layouts: 5.96 us -> 7.9 us
  transfers between devices with their start and end apart: 6 -> 7, of which waited for: 4 -> 3; matrix products, arithmetic and copies ran while one was open for 9% -> 16% of each run, Pallas kernels for 30% -> 32%
where the time goes in v4:
time: 167 us
  Pallas kernels  72.1 us (43%)
  waiting for transfers between devices  33.2 us (20%)
  matrix products  16.8 us (10%)
  local copies, waits for them, and re-layouts  16.5 us (10%)
  between operations  13.5 us (8%)
  starting transfers between devices  10.5 us (6%)
  other arithmetic  4.35 us (3%)
    pallas_call x1, Pallas kernels, on_device(): pl.pallas_call(chain_kernel, out_shape=[like((STATE, INNER), BF16)] * 2,...  28.3 us
    pallas_call x1, Pallas kernels, on_device(): pl.pallas_call(finish_kernel, grid=(spans,), in_specs=[strip(INNER)] * 2...  18.3 us
    pallas_call x1, Pallas kernels, on_device(): pl.pallas_call(states_kernel, out_shape=[like((length, CONVW), BF16)] * 2...  17.8 us
    ppermute x1, waiting for transfers between devices, on_device(): got = lax.ppermute(jnp.where(odd, ahead_half, reverse_half), 'seq', swap)  11.9 us
    ppermute x1, waiting for transfers between devices, on_device(): back = lax.ppermute(jnp.where(odd, first, second), 'seq', swap)  10.7 us
    all_gather x1, waiting for transfers between devices, on_device(): weight = lax.all_gather(in_weight[:, INNER:], 'batch', axis=0, tiled=True)  10.5 us
    unnamed x44, local copies, waits for them, and re-layouts  7.9 us
    pallas_call x1, Pallas kernels, on_device(): pl.pallas_call(within_kernel, grid=(spans,), in_specs=[strip(CONVW)] * 2...  7.68 us
  transfers between devices with their start and end apart: 7, of which 3 were waited for; matrix products, arithmetic and copies ran while one was open for 16% of the time, Pallas kernels for 32%

profile of v4, /device:TPU:0, one launch (start us, length us, event | category | flops | bytes accessed | tf_op | source)
XLA Modules:
  0.0 166.9 jit_solution(13916627795871223830)
XLA Ops:
  6.5 2.5 %slice.39 = bf16[256,2304]{1,0:T(8,128)(2,1)} slice(bf16[256,4352]{1,0:T(8,128)(2,1)} %param.11), slice={[0:256], [2048:4352]} | slice | bytes 2359296 | tf_op jit(solution)/shard_map/slice | solution.py:269
  9.2 3.0 %collective-permute-start = (bf16[256,1024]{1,0:T(8,128)(2,1)S(1)}, bf16[256,1024]{1,0:T(8,128)(2,1)S(1)}, u32[]{:S(2)}, u32[]{:S(2)}) collective-permute-start(bf16[256,1024]{1,0:T(8,128)(2,1)S(1)} %select_bitcast_fusion), channel_id=1, source_target_pairs={{0,4},{4,0},{8,12},{12,8},{16,20},{20,16},{24,28},{28,24},{1,5},{5... | collective-permute-start | bytes 1572872 | tf_op jit(solution)/shard_map/ppermute | solution.py:273
  12.2 11.9 %collective-permute-done = bf16[256,1024]{1,0:T(8,128)(2,1)S(1)} collective-permute-done((bf16[256,1024]{1,0:T(8,128)(2,1)S(1)}, bf16[256,1024]{1,0:T(8,128)(2,1)S(1)}, u32[]{:S(2)}, u32[]{:S(2)}) %collective-permute-start) | collective-permute-done | bytes 524320 | tf_op jit(solution)/shard_map/ppermute | solution.py:273
  24.3 1.3 collective-permute-start.2
  25.6 4.5 %collective-permute-start.1 = (bf16[16,1024]{1,0:T(8,128)(2,1)S(1)}, bf16[16,1024]{1,0:T(8,128)(2,1)S(1)}, u32[]{:S(2)}, u32[]{:S(2)}) collective-permute-start(bf16[16,1024]{1,0:T(8,128)(2,1)S(1)} %slice.45), channel_id=1, source_target_pairs={{0,8},{4,12},{8,16},{12,20},{16,24},{20,28},{1,9},{5,13},{9,17},{1... | collective-permute-start | bytes 98312 | tf_op jit(solution)/shard_map/ppermute | solution.py:275
  30.1 2.3 %slice.34 = bf16[256,2048]{1,0:T(8,128)(2,1)} slice(bf16[256,4352]{1,0:T(8,128)(2,1)} %param.11), slice={[0:256], [0:2048]} | slice | bytes 2097152 | tf_op jit(solution)/shard_map/slice | solution.py:278
  32.4 1.1 pad_maximum_fusion
  33.7 2.6 %fusion.6 = bf16[544,1024]{1,0:T(8,128)(2,1)S(1)} fusion(bf16[544,1024]{1,0:T(8,128)(2,1)} %pad_maximum_fusion, pred[]{:T(512)S(6)} %eq.14), kind=kOutput, calls=%fused_computation.9 | convolution fusion | flops 1145602048 | bytes 2228225 | tf_op jit(solution)/shard_map/dot_general | solution.py:284
  36.3 1.1 compare_select_fusion
  38.8 10.5 %all-gather.4.cloned.1.call-done = bf16[1024,2304]{1,0:T(8,128)(2,1)} async-done(((bf16[256,2304]{1,0:T(8,128)(2,1)}), bf16[1024,2304]{1,0:T(8,128)(2,1)}) %all-gather.4.cloned.1.call-update) | async-done | bytes 4718608 | tf_op jit(solution)/shard_map/all_gather | solution.py:269
  49.4 6.3 %convolution_convert_fusion.proj = bf16[544,2304]{1,0:T(8,128)(2,1)} fusion(bf16[544,1024]{1,0:T(8,128)(2,1)S(1)} %fusion.6, bf16[1024,2304]{1,0:T(8,128)(2,1)} %all-gather.4.cloned.1.call-done), kind=kOutput, calls=%fused_computation | convolution fusion | flops 2568167424 | bytes 8339456 | tf_op jit(solution)/shard_map/dot_general | solution.py:304
  55.7 17.8 %states.1 = (bf16[512,2304]{1,0:T(8,128)(2,1)S(1)}, bf16[512,2304]{1,0:T(8,128)(2,1)}, f32[512,2048]{1,0:T(8,128)}, f32[512,2048]{1,0:T(8,128)}, f32[128,2048]{1,0:T(8,128)S(1)}, /*index=5*/f32[128,2048]{1,0:T(8,128)S(1)}) custom-call(bf16[544,2304]{1,0:T(8,128)(2,1)} %convolution_convert_fusion.proj, f32[4,2304]{1,0:T(4,128)S(1)} %copy-done.14, ...), custom_call_target="tpu_custom_call" | custom-call | flops 8000000000 | bytes 20000000 | tf_op jit(solution)/shard_map/states/pallas_call | solution.py:305
  76.5 1.6 fusion.1.turn
  80.1 1.2 copy-done.5
  81.4 1.2 copy-done.7
  82.6 28.3 %chain.1 = (bf16[128,2048]{1,0:T(8,128)(2,1)S(1)}, bf16[128,2048]{1,0:T(8,128)(2,1)S(1)}) custom-call(f32[128,2048]{1,0:T(8,128)S(1)} %copy-done.5, f32[128,2048]{1,0:T(8,128)S(1)} %copy-done.7, f32[1,2048]{1,0:T(1,128)S(1)} %broadcast_in_dim.32.decay_f, f32[1,2048]{1,0:T(1,128)S(1)} %broadcast_in_dim.33.decay_b), custom_call_target="tpu_custom_call" | custom-call | flops 2000000 | bytes 8000000 | tf_op jit(solution)/shard_map/chain/pallas_call | solution.py:320
  111.7 6.5 %convolution_convert_fusion.1.gate = bf16[512,2048]{1,0:T(8,128)(2,1)} fusion(bf16[1024,2048]{1,0:T(8,128)(2,1)} %all-gather.6.cloned.1.call-done, bf16[544,1024]{1,0:T(8,128)(2,1)} %copy-done.21), kind=kOutput, calls=%fused_computation.4 | convolution fusion | flops 2148532224 | bytes 7340032 | tf_op jit(solution)/shard_map/dot_general | solution.py:339
  118.3 7.7 %within.1 = (f32[512,2048]{1,0:T(8,128)}, f32[512,2048]{1,0:T(8,128)}) custom-call(bf16[512,2304]{1,0:T(8,128)(2,1)S(1)} %get-tuple-element.22.act_f.read_f, bf16[512,2304]{1,0:T(8,128)(2,1)S(1)} %copy-done.2, f32[512,32]{1,0:T(8,128)S(1)} %bitcast.58, f32[512,32]{1,0:T(8,128)S(1)} %bitcast.61, f32[32,512]{1,0:T(8,128)S(1)} %copy-done.10, ...), custom_call_target="tpu_custom_call" | custom-call | flops 24999999488 | bytes 15000000 | tf_op jit(solution)/shard_map/within/pallas_call | solution.py:341
  125.9 1.6 copy-done.3
  127.5 1.0 copy-done.9
  128.6 18.3 %finish.1 = bf16[512,1024]{1,0:T(8,128)(2,1)S(1)} custom-call(f32[512,2048]{1,0:T(8,128)} %get-tuple-element.24.y_f, f32[512,2048]{1,0:T(8,128)} %get-tuple-element.25.y_b, bf16[512,2048]{1,0:T(8,128)(2,1)S(1)} %copy-done.3, bf16[512,2304]{1,0:T(8,128)(2,1)} %copy-done.1, bf16[512,2304]{1,0:T(8,128)(2,1)} %get-tuple-element.23.act_b.read_b, ...), custom_call_target="tpu_custom_call" | custom-call | flops 8000000000 | bytes 20000000 | tf_op jit(solution)/shard_map/finish/pallas_call | solution.py:352
  147.0 1.5 collective-permute-start.3
  148.5 10.7 %collective-permute-done.3 = bf16[256,1024]{1,0:T(8,128)(2,1)S(1)} collective-permute-done((bf16[256,1024]{1,0:T(8,128)(2,1)S(1)}, bf16[256,1024]{1,0:T(8,128)(2,1)S(1)}, u32[]{:S(2)}, u32[]{:S(2)}) %collective-permute-start.3) | collective-permute-done | bytes 524320 | tf_op jit(solution)/shard_map/ppermute | solution.py:378
  159.3 1.1 maximum_bitcast_fusion
  (81 shorter events, 7.6 us)
Async XLA Ops:
  6.5 29.7 %copy-start = (bf16[1024,32]{0,1:T(8,128)(2,1)S(1)}, bf16[1024,32]{0,1:T(8,128)(2,1)}, u32[]{:S(2)}) copy-start(bf16[1024,32]{0,1:T(8,128)(2,1)} %param.12) | copy-start | bytes 196612
  6.5 2.6 %copy-start.16 = (bf16[1,256,2048]{2,1,0:T(8,128)(2,1)S(1)}, bf16[1,256,2048]{2,1,0:T(8,128)(2,1)}, u32[]{:S(2)}) copy-start(bf16[1,256,2048]{2,1,0:T(8,128)(2,1)} %param.10) | copy-start | bytes 3145732
  6.5 42.8 %all-gather.4.cloned.1.call-start = ((), (), s32[]{:S(2)}) async-start(), calls=%async_computation | async-start | bytes 5898240 | tf_op jit(solution)/shard_map/all_gather | solution.py:269
  9.1 102.7 %all-gather.6.cloned.1.call-start = ((), (), s32[]{:S(2)}) async-start(), calls=%async_computation.1 | async-start | bytes 5242880 | tf_op jit(solution)/shard_map/all_gather | solution.py:279
  9.2 14.9 %collective-permute-start = (bf16[256,1024]{1,0:T(8,128)(2,1)S(1)}, bf16[256,1024]{1,0:T(8,128)(2,1)S(1)}, u32[]{:S(2)}, u32[]{:S(2)}) collective-permute-start(bf16[256,1024]{1,0:T(8,128)(2,1)S(1)} %select_bitcast_fusion), channel_id=1, source_target_pairs={{0,4},{4,0},{8,12},{12,8},{16,20},{20,16},{24,28},{28,24},{1,5},{5... | collective-permute-start | bytes 1572872 | tf_op jit(solution)/shard_map/ppermute | solution.py:273
  24.2 9.4 %copy-start.17 = (f32[2304]{0:T(1024)S(1)}, f32[2304]{0:T(1024)}, u32[]{:S(2)}) copy-start(f32[2304]{0:T(1024)} %param.14) | copy-start | bytes 27652
  24.2 9.4 %copy-start.19 = (f32[32]{0:T(128)S(1)}, f32[32]{0:T(128)}, u32[]{:S(2)}) copy-start(f32[32]{0:T(128)} %param.16) | copy-start | bytes 388
  24.3 8.2 %collective-permute-start.2 = (bf16[16,1024]{1,0:T(8,128)(2,1)S(1)}, bf16[16,1024]{1,0:T(8,128)(2,1)S(1)}, u32[]{:S(2)}, u32[]{:S(2)}) collective-permute-start(bf16[16,1024]{1,0:T(8,128)(2,1)S(1)} %slice.46), channel_id=1, source_target_pairs={{8,0},{12,4},{16,8},{20,12},{24,16},{28,20},{9,1},{13,5},{17,9},{2... | collective-permute-start | bytes 98312 | tf_op jit(solution)/shard_map/ppermute | solution.py:276
  25.6 6.9 %collective-permute-start.1 = (bf16[16,1024]{1,0:T(8,128)(2,1)S(1)}, bf16[16,1024]{1,0:T(8,128)(2,1)S(1)}, u32[]{:S(2)}, u32[]{:S(2)}) collective-permute-start(bf16[16,1024]{1,0:T(8,128)(2,1)S(1)} %slice.45), channel_id=1, source_target_pairs={{0,8},{4,12},{8,16},{12,20},{16,24},{20,28},{1,9},{5,13},{9,17},{1... | collective-permute-start | bytes 98312 | tf_op jit(solution)/shard_map/ppermute | solution.py:275
  33.6 92.4 %all-gather.8.cloned.1.call-start = ((), (), s32[]{:S(2)}) async-start(), calls=%async_computation.2 | async-start | bytes 5242880 | tf_op jit(solution)/shard_map/all_gather | solution.py:319
  33.7 2.6 %copy-start.20 = (f32[32]{0:T(128)S(1)}, f32[32]{0:T(128)}, u32[]{:S(2)}) copy-start(f32[32]{0:T(128)} %param.15) | copy-start | bytes 388
  36.3 19.4 %copy-start.21 = (bf16[544,1024]{1,0:T(8,128)(2,1)}, bf16[544,1024]{1,0:T(8,128)(2,1)S(1)}, u32[]{:S(2)}) copy-start(bf16[544,1024]{1,0:T(8,128)(2,1)S(1)} %fusion.6) | copy-start | bytes 3342340
  38.8 16.9 %copy-start.14 = (f32[4,2304]{1,0:T(4,128)S(1)}, f32[4,2304]{1,0:T(4,128)}, u32[]{:S(2)}) copy-start(f32[4,2304]{1,0:T(4,128)} %weight.1) | copy-start | bytes 110596
  55.7 19.8 %copy-start.18 = (f32[32]{0:T(128)S(1)}, f32[32]{0:T(128)}, u32[]{:S(2)}) copy-start(f32[32]{0:T(128)} %param.17) | copy-start | bytes 388
  75.5 42.7 %copy-start.1 = (bf16[512,2304]{1,0:T(8,128)(2,1)}, bf16[512,2304]{1,0:T(8,128)(2,1)S(1)}, u32[]{:S(2)}) copy-start(bf16[512,2304]{1,0:T(8,128)(2,1)S(1)} %get-tuple-element.22.act_f.read_f) | copy-start | bytes 7077892
  81.4 1.2 copy-start.7
  111.7 6.5 %copy-start.2 = (bf16[512,2304]{1,0:T(8,128)(2,1)S(1)}, bf16[512,2304]{1,0:T(8,128)(2,1)}, u32[]{:S(2)}) copy-start(bf16[512,2304]{1,0:T(8,128)(2,1)} %get-tuple-element.23.act_b.read_b) | copy-start | bytes 7077892
  111.7 6.5 %copy-start.10 = (f32[32,512]{1,0:T(8,128)S(1)}, f32[32,512]{1,0:T(8,128)}, u32[]{:S(2)}) copy-start(f32[32,512]{1,0:T(8,128)} %copy.29.row_f) | copy-start | bytes 196612
  111.7 6.5 %copy-start.11 = (f32[32,512]{1,0:T(8,128)S(1)}, f32[32,512]{1,0:T(8,128)}, u32[]{:S(2)}) copy-start(f32[32,512]{1,0:T(8,128)} %copy.30.row_b) | copy-start | bytes 196612
  111.7 6.5 %copy-start.13 = (f32[1,2048]{1,0:T(1,128)S(1)}, f32[1,2048]{1,0:T(1,128)}, u32[]{:S(2)}) copy-start(f32[1,2048]{1,0:T(1,128)} %broadcast_in_dim_reshape.3.skip) | copy-start | bytes 24580
  111.7 6.5 %copy-start.15 = (f32[32,512]{1,0:T(8,128)S(1)}, f32[32,512]{1,0:T(8,128)}, u32[]{:S(2)}) copy-start(f32[32,512]{1,0:T(8,128)} %get-tuple-element.49.row_dt) | copy-start | bytes 196612
  118.2 7.7 %copy-start.12 = (f32[2048]{0:T(1024)S(1)}, f32[2048]{0:T(1024)}, u32[]{:S(2)}) copy-start(f32[2048]{0:T(1024)} %param.18) | copy-start | bytes 24580
  125.9 1.6 copy-start.3
  147.0 12.2 %collective-permute-start.3 = (bf16[256,1024]{1,0:T(8,128)(2,1)S(1)}, bf16[256,1024]{1,0:T(8,128)(2,1)S(1)}, u32[]{:S(2)}, u32[]{:S(2)}) collective-permute-start(bf16[256,1024]{1,0:T(8,128)(2,1)S(1)} %broadcast_select_fusion.4), channel_id=1, source_target_pairs={{0,4},{4,0},{8,12},{12,8},{16,20},{20,16},{24,28},{28,24},{1,5},{5... | collective-permute-start | bytes 1572872 | tf_op jit(solution)/shard_map/ppermute | solution.py:378
  (5 other events, 5.0 us)
Sparse Core Ops, SparseCore 0:
  9.2 40.1 all-gather.3
  50.9 34.4 all-gather.5
  87.0 34.4 all-gather.7

commit v5 on v4

--- a/solution.py
+++ b/solution.py
@@ -13,7 +13,7 @@
 PAIRS = INNER // 128
 CONVW = INNER + 2 * STATE
 EDGE = 16
-PIECES = 4
+PIECES = 8
 MESH = pl.DeviceIdType.MESH
 F32 = jnp.float32
 BF16 = jnp.bfloat16

time: 167 us -> 173 us (1.036)
  Pallas kernels: 72.1 us -> 80.2 us
  waiting for transfers between devices: 33.2 us -> 30.2 us
    pallas_call x1, Pallas kernels: 28.3 us -> 36.4 us  [on_device(): pl.pallas_call(chain_kernel, out_shape=[like((STATE, INNER), BF16)] * 2,...]
    ppermute x1, waiting for transfers between devices: 10.7 us -> 7.73 us  [on_device(): back = lax.ppermute(jnp.where(odd, first, second), 'seq', swap)]
  transfers between devices with their start and end apart: 7 -> 7, of which waited for: 3 -> 3; matrix products, arithmetic and copies ran while one was open for 16% -> 15% of each run, Pallas kernels for 32% -> 36%
where the time goes in v5:
time: 173 us; the launch traced here: 172 us
  Pallas kernels  80.2 us (46%)
  waiting for transfers between devices  30.2 us (17%)
  matrix products  16.8 us (10%)
  local copies, waits for them, and re-layouts  16.5 us (10%)
  between operations  13.5 us (8%)
  starting transfers between devices  10.5 us (6%)
  other arithmetic  4.35 us (3%)
    pallas_call x1, Pallas kernels, on_device(): pl.pallas_call(chain_kernel, out_shape=[like((STATE, INNER), BF16)] * 2,...  36.4 us
    pallas_call x1, Pallas kernels, on_device(): pl.pallas_call(finish_kernel, grid=(spans,), in_specs=[strip(INNER)] * 2...  18.3 us
    pallas_call x1, Pallas kernels, on_device(): pl.pallas_call(states_kernel, out_shape=[like((length, CONVW), BF16)] * 2...  17.8 us
    ppermute x1, waiting for transfers between devices, on_device(): got = lax.ppermute(jnp.where(odd, ahead_half, reverse_half), 'seq', swap)  11.9 us
    all_gather x1, waiting for transfers between devices, on_device(): weight = lax.all_gather(in_weight[:, INNER:], 'batch', axis=0, tiled=True)  10.5 us
    unnamed x44, local copies, waits for them, and re-layouts  7.9 us
    ppermute x1, waiting for transfers between devices, on_device(): back = lax.ppermute(jnp.where(odd, first, second), 'seq', swap)  7.73 us
    pallas_call x1, Pallas kernels, on_device(): pl.pallas_call(within_kernel, grid=(spans,), in_specs=[strip(CONVW)] * 2...  7.68 us
  transfers between devices with their start and end apart: 7, of which 3 were waited for; matrix products, arithmetic and copies ran while one was open for 15% of the time, Pallas kernels for 36%

profile of v5, /device:TPU:0, one launch (start us, length us, event | category | flops | bytes accessed | tf_op | source)
XLA Modules:
  0.0 172.0 jit_solution(12453607451169676602)
XLA Ops:
  6.5 2.5 %slice.39 = bf16[256,2304]{1,0:T(8,128)(2,1)} slice(bf16[256,4352]{1,0:T(8,128)(2,1)} %param.11), slice={[0:256], [2048:4352]} | slice | bytes 2359296 | tf_op jit(solution)/shard_map/slice | solution.py:269
  9.2 3.0 %collective-permute-start = (bf16[256,1024]{1,0:T(8,128)(2,1)S(1)}, bf16[256,1024]{1,0:T(8,128)(2,1)S(1)}, u32[]{:S(2)}, u32[]{:S(2)}) collective-permute-start(bf16[256,1024]{1,0:T(8,128)(2,1)S(1)} %select_bitcast_fusion), channel_id=1, source_target_pairs={{0,4},{4,0},{8,12},{12,8},{16,20},{20,16},{24,28},{28,24},{1,5},{5... | collective-permute-start | bytes 1572872 | tf_op jit(solution)/shard_map/ppermute | solution.py:273
  12.2 11.9 %collective-permute-done = bf16[256,1024]{1,0:T(8,128)(2,1)S(1)} collective-permute-done((bf16[256,1024]{1,0:T(8,128)(2,1)S(1)}, bf16[256,1024]{1,0:T(8,128)(2,1)S(1)}, u32[]{:S(2)}, u32[]{:S(2)}) %collective-permute-start) | collective-permute-done | bytes 524320 | tf_op jit(solution)/shard_map/ppermute | solution.py:273
  24.3 1.3 collective-permute-start.2
  25.6 4.5 %collective-permute-start.1 = (bf16[16,1024]{1,0:T(8,128)(2,1)S(1)}, bf16[16,1024]{1,0:T(8,128)(2,1)S(1)}, u32[]{:S(2)}, u32[]{:S(2)}) collective-permute-start(bf16[16,1024]{1,0:T(8,128)(2,1)S(1)} %slice.45), channel_id=1, source_target_pairs={{0,8},{4,12},{8,16},{12,20},{16,24},{20,28},{1,9},{5,13},{9,17},{1... | collective-permute-start | bytes 98312 | tf_op jit(solution)/shard_map/ppermute | solution.py:275
  30.1 2.3 %slice.34 = bf16[256,2048]{1,0:T(8,128)(2,1)} slice(bf16[256,4352]{1,0:T(8,128)(2,1)} %param.11), slice={[0:256], [0:2048]} | slice | bytes 2097152 | tf_op jit(solution)/shard_map/slice | solution.py:278
  32.4 1.1 pad_maximum_fusion
  33.7 2.6 %fusion.6 = bf16[544,1024]{1,0:T(8,128)(2,1)S(1)} fusion(bf16[544,1024]{1,0:T(8,128)(2,1)} %pad_maximum_fusion, pred[]{:T(512)S(6)} %eq.14), kind=kOutput, calls=%fused_computation.9 | convolution fusion | flops 1145602048 | bytes 2228225 | tf_op jit(solution)/shard_map/dot_general | solution.py:284
  36.3 1.1 compare_select_fusion
  38.8 10.5 %all-gather.4.cloned.1.call-done = bf16[1024,2304]{1,0:T(8,128)(2,1)} async-done(((bf16[256,2304]{1,0:T(8,128)(2,1)}), bf16[1024,2304]{1,0:T(8,128)(2,1)}) %all-gather.4.cloned.1.call-update) | async-done | bytes 4718608 | tf_op jit(solution)/shard_map/all_gather | solution.py:269
  49.4 6.3 %convolution_convert_fusion.proj = bf16[544,2304]{1,0:T(8,128)(2,1)} fusion(bf16[544,1024]{1,0:T(8,128)(2,1)S(1)} %fusion.6, bf16[1024,2304]{1,0:T(8,128)(2,1)} %all-gather.4.cloned.1.call-done), kind=kOutput, calls=%fused_computation | convolution fusion | flops 2568167424 | bytes 8339456 | tf_op jit(solution)/shard_map/dot_general | solution.py:304
  55.7 17.8 %states.1 = (bf16[512,2304]{1,0:T(8,128)(2,1)S(1)}, bf16[512,2304]{1,0:T(8,128)(2,1)}, f32[512,2048]{1,0:T(8,128)}, f32[512,2048]{1,0:T(8,128)}, f32[128,2048]{1,0:T(8,128)S(1)}, /*index=5*/f32[128,2048]{1,0:T(8,128)S(1)}) custom-call(bf16[544,2304]{1,0:T(8,128)(2,1)} %convolution_convert_fusion.proj, f32[4,2304]{1,0:T(4,128)S(1)} %copy-done.14, ...), custom_call_target="tpu_custom_call" | custom-call | flops 8000000000 | bytes 20000000 | tf_op jit(solution)/shard_map/states/pallas_call | solution.py:305
  76.5 1.6 fusion.1.turn
  80.1 1.2 copy-done.5
  81.4 1.2 copy-done.7
  82.6 36.4 %chain.1 = (bf16[128,2048]{1,0:T(8,128)(2,1)S(1)}, bf16[128,2048]{1,0:T(8,128)(2,1)S(1)}) custom-call(f32[128,2048]{1,0:T(8,128)S(1)} %copy-done.5, f32[128,2048]{1,0:T(8,128)S(1)} %copy-done.7, f32[1,2048]{1,0:T(1,128)S(1)} %broadcast_in_dim.32.decay_f, f32[1,2048]{1,0:T(1,128)S(1)} %broadcast_in_dim.33.decay_b), custom_call_target="tpu_custom_call" | custom-call | flops 2000000 | bytes 8000000 | tf_op jit(solution)/shard_map/chain/pallas_call | solution.py:320
  119.9 6.5 %convolution_convert_fusion.1.gate = bf16[512,2048]{1,0:T(8,128)(2,1)} fusion(bf16[1024,2048]{1,0:T(8,128)(2,1)} %all-gather.6.cloned.1.call-done, bf16[544,1024]{1,0:T(8,128)(2,1)} %copy-done.21), kind=kOutput, calls=%fused_computation.4 | convolution fusion | flops 2148532224 | bytes 7340032 | tf_op jit(solution)/shard_map/dot_general | solution.py:339
  126.4 7.7 %within.1 = (f32[512,2048]{1,0:T(8,128)}, f32[512,2048]{1,0:T(8,128)}) custom-call(bf16[512,2304]{1,0:T(8,128)(2,1)S(1)} %get-tuple-element.22.act_f.read_f, bf16[512,2304]{1,0:T(8,128)(2,1)S(1)} %copy-done.2, f32[512,32]{1,0:T(8,128)S(1)} %bitcast.58, f32[512,32]{1,0:T(8,128)S(1)} %bitcast.61, f32[32,512]{1,0:T(8,128)S(1)} %copy-done.10, ...), custom_call_target="tpu_custom_call" | custom-call | flops 24999999488 | bytes 15000000 | tf_op jit(solution)/shard_map/within/pallas_call | solution.py:341
  134.1 1.6 copy-done.3
  135.6 1.0 copy-done.9
  136.7 18.3 %finish.1 = bf16[512,1024]{1,0:T(8,128)(2,1)S(1)} custom-call(f32[512,2048]{1,0:T(8,128)} %get-tuple-element.24.y_f, f32[512,2048]{1,0:T(8,128)} %get-tuple-element.25.y_b, bf16[512,2048]{1,0:T(8,128)(2,1)S(1)} %copy-done.3, bf16[512,2304]{1,0:T(8,128)(2,1)} %copy-done.1, bf16[512,2304]{1,0:T(8,128)(2,1)} %get-tuple-element.23.act_b.read_b, ...), custom_call_target="tpu_custom_call" | custom-call | flops 8000000000 | bytes 20000000 | tf_op jit(solution)/shard_map/finish/pallas_call | solution.py:352
  155.1 1.5 collective-permute-start.3
  156.6 7.7 %collective-permute-done.3 = bf16[256,1024]{1,0:T(8,128)(2,1)S(1)} collective-permute-done((bf16[256,1024]{1,0:T(8,128)(2,1)S(1)}, bf16[256,1024]{1,0:T(8,128)(2,1)S(1)}, u32[]{:S(2)}, u32[]{:S(2)}) %collective-permute-start.3) | collective-permute-done | bytes 524320 | tf_op jit(solution)/shard_map/ppermute | solution.py:378
  164.4 1.1 maximum_bitcast_fusion
  (81 shorter events, 7.6 us)
Async XLA Ops:
  6.5 29.7 %copy-start = (bf16[1024,32]{0,1:T(8,128)(2,1)S(1)}, bf16[1024,32]{0,1:T(8,128)(2,1)}, u32[]{:S(2)}) copy-start(bf16[1024,32]{0,1:T(8,128)(2,1)} %param.12) | copy-start | bytes 196612
  6.5 2.6 %copy-start.16 = (bf16[1,256,2048]{2,1,0:T(8,128)(2,1)S(1)}, bf16[1,256,2048]{2,1,0:T(8,128)(2,1)}, u32[]{:S(2)}) copy-start(bf16[1,256,2048]{2,1,0:T(8,128)(2,1)} %param.10) | copy-start | bytes 3145732
  6.5 42.8 %all-gather.4.cloned.1.call-start = ((), (), s32[]{:S(2)}) async-start(), calls=%async_computation | async-start | bytes 5898240 | tf_op jit(solution)/shard_map/all_gather | solution.py:269
  9.1 110.8 %all-gather.6.cloned.1.call-start = ((), (), s32[]{:S(2)}) async-start(), calls=%async_computation.1 | async-start | bytes 5242880 | tf_op jit(solution)/shard_map/all_gather | solution.py:279
  9.2 14.9 %collective-permute-start = (bf16[256,1024]{1,0:T(8,128)(2,1)S(1)}, bf16[256,1024]{1,0:T(8,128)(2,1)S(1)}, u32[]{:S(2)}, u32[]{:S(2)}) collective-permute-start(bf16[256,1024]{1,0:T(8,128)(2,1)S(1)} %select_bitcast_fusion), channel_id=1, source_target_pairs={{0,4},{4,0},{8,12},{12,8},{16,20},{20,16},{24,28},{28,24},{1,5},{5... | collective-permute-start | bytes 1572872 | tf_op jit(solution)/shard_map/ppermute | solution.py:273
  24.2 9.4 %copy-start.17 = (f32[2304]{0:T(1024)S(1)}, f32[2304]{0:T(1024)}, u32[]{:S(2)}) copy-start(f32[2304]{0:T(1024)} %param.14) | copy-start | bytes 27652
  24.2 9.4 %copy-start.19 = (f32[32]{0:T(128)S(1)}, f32[32]{0:T(128)}, u32[]{:S(2)}) copy-start(f32[32]{0:T(128)} %param.16) | copy-start | bytes 388
  24.3 8.2 %collective-permute-start.2 = (bf16[16,1024]{1,0:T(8,128)(2,1)S(1)}, bf16[16,1024]{1,0:T(8,128)(2,1)S(1)}, u32[]{:S(2)}, u32[]{:S(2)}) collective-permute-start(bf16[16,1024]{1,0:T(8,128)(2,1)S(1)} %slice.46), channel_id=1, source_target_pairs={{8,0},{12,4},{16,8},{20,12},{24,16},{28,20},{9,1},{13,5},{17,9},{2... | collective-permute-start | bytes 98312 | tf_op jit(solution)/shard_map/ppermute | solution.py:276
  25.6 6.9 %collective-permute-start.1 = (bf16[16,1024]{1,0:T(8,128)(2,1)S(1)}, bf16[16,1024]{1,0:T(8,128)(2,1)S(1)}, u32[]{:S(2)}, u32[]{:S(2)}) collective-permute-start(bf16[16,1024]{1,0:T(8,128)(2,1)S(1)} %slice.45), channel_id=1, source_target_pairs={{0,8},{4,12},{8,16},{12,20},{16,24},{20,28},{1,9},{5,13},{9,17},{1... | collective-permute-start | bytes 98312 | tf_op jit(solution)/shard_map/ppermute | solution.py:275
  33.6 100.5 %all-gather.8.cloned.1.call-start = ((), (), s32[]{:S(2)}) async-start(), calls=%async_computation.2 | async-start | bytes 5242880 | tf_op jit(solution)/shard_map/all_gather | solution.py:319
  33.7 2.6 %copy-start.20 = (f32[32]{0:T(128)S(1)}, f32[32]{0:T(128)}, u32[]{:S(2)}) copy-start(f32[32]{0:T(128)} %param.15) | copy-start | bytes 388
  36.3 19.4 %copy-start.21 = (bf16[544,1024]{1,0:T(8,128)(2,1)}, bf16[544,1024]{1,0:T(8,128)(2,1)S(1)}, u32[]{:S(2)}) copy-start(bf16[544,1024]{1,0:T(8,128)(2,1)S(1)} %fusion.6) | copy-start | bytes 3342340
  38.8 16.9 %copy-start.14 = (f32[4,2304]{1,0:T(4,128)S(1)}, f32[4,2304]{1,0:T(4,128)}, u32[]{:S(2)}) copy-start(f32[4,2304]{1,0:T(4,128)} %weight.1) | copy-start | bytes 110596
  55.7 19.8 %copy-start.18 = (f32[32]{0:T(128)S(1)}, f32[32]{0:T(128)}, u32[]{:S(2)}) copy-start(f32[32]{0:T(128)} %param.17) | copy-start | bytes 388
  75.5 50.8 %copy-start.1 = (bf16[512,2304]{1,0:T(8,128)(2,1)}, bf16[512,2304]{1,0:T(8,128)(2,1)S(1)}, u32[]{:S(2)}) copy-start(bf16[512,2304]{1,0:T(8,128)(2,1)S(1)} %get-tuple-element.22.act_f.read_f) | copy-start | bytes 7077892
  81.4 1.2 copy-start.7
  119.8 6.5 %copy-start.2 = (bf16[512,2304]{1,0:T(8,128)(2,1)S(1)}, bf16[512,2304]{1,0:T(8,128)(2,1)}, u32[]{:S(2)}) copy-start(bf16[512,2304]{1,0:T(8,128)(2,1)} %get-tuple-element.23.act_b.read_b) | copy-start | bytes 7077892
  119.8 6.5 %copy-start.10 = (f32[32,512]{1,0:T(8,128)S(1)}, f32[32,512]{1,0:T(8,128)}, u32[]{:S(2)}) copy-start(f32[32,512]{1,0:T(8,128)} %copy.29.row_f) | copy-start | bytes 196612
  119.8 6.5 %copy-start.11 = (f32[32,512]{1,0:T(8,128)S(1)}, f32[32,512]{1,0:T(8,128)}, u32[]{:S(2)}) copy-start(f32[32,512]{1,0:T(8,128)} %copy.30.row_b) | copy-start | bytes 196612
  119.8 6.5 %copy-start.13 = (f32[1,2048]{1,0:T(1,128)S(1)}, f32[1,2048]{1,0:T(1,128)}, u32[]{:S(2)}) copy-start(f32[1,2048]{1,0:T(1,128)} %broadcast_in_dim_reshape.3.skip) | copy-start | bytes 24580
  119.8 6.5 %copy-start.15 = (f32[32,512]{1,0:T(8,128)S(1)}, f32[32,512]{1,0:T(8,128)}, u32[]{:S(2)}) copy-start(f32[32,512]{1,0:T(8,128)} %get-tuple-element.49.row_dt) | copy-start | bytes 196612
  126.4 7.7 %copy-start.12 = (f32[2048]{0:T(1024)S(1)}, f32[2048]{0:T(1024)}, u32[]{:S(2)}) copy-start(f32[2048]{0:T(1024)} %param.18) | copy-start | bytes 24580
  134.1 1.6 copy-start.3
  155.1 9.2 %collective-permute-start.3 = (bf16[256,1024]{1,0:T(8,128)(2,1)S(1)}, bf16[256,1024]{1,0:T(8,128)(2,1)S(1)}, u32[]{:S(2)}, u32[]{:S(2)}) collective-permute-start(bf16[256,1024]{1,0:T(8,128)(2,1)S(1)} %broadcast_select_fusion.4), channel_id=1, source_target_pairs={{0,4},{4,0},{8,12},{12,8},{16,20},{20,16},{24,28},{28,24},{1,5},{5... | collective-permute-start | bytes 1572872 | tf_op jit(solution)/shard_map/ppermute | solution.py:378
  (5 other events, 5.0 us)
Sparse Core Ops, SparseCore 0:
  9.2 40.1 all-gather.3
  50.9 34.4 all-gather.5
  87.0 34.4 all-gather.7
